TPU v7x, 512 devices: a whole 4x4x16 slice. The times are simulated.
512 devices in a mesh: row: 32 (over z_lo, y), col: 16 (over z_hi, x, core).
Axes of the slice: x: 4, y: 4, z: 16 (z_hi: 2, z_lo: 8; z = z_hi * 8 + z_lo), core: 2. Of those that a mesh axis runs over, the one named last changes fastest.
Arguments:
- water_depth: float32 [2048, 2048], P('row', 'col'), may hold values from 1 to 2
- discharge: float32 [2, 2048, 2048], P(None, 'row', 'col'), may hold values from -1.5 to 1.5
- sediment: float32 [4, 2048, 2048], P(None, 'row', 'col'), may hold values from 0.01 to 0.1
- bed_level: float32 [512, 512], P(('row', 'col')), may hold values from -3 to 3
- cell_map: int32 [2048, 2048], P('row', 'col'), may hold values from 0 to 8191, as said below
- wet_mask: int32 [2048, 2048], P('row', 'col'), may hold values 0 or 1
- sediment_params: float32 [3, 4], replicated, may hold values from 0.5 to 2
Outputs:
- depth_out: float32 [2048, 2048], P('row', 'col')
- discharge_out: float32 [2, 2048, 2048], P(None, 'row', 'col')
- sediment_out: float32 [4, 2048, 2048], P(None, 'row', 'col')
- fine_bed: float32 [2048, 2048], P('row', 'col')
- bed_out: float32 [512, 512], P(('row', 'col'))
- deposit: float32 [4, 512, 512], P(None, ('row', 'col'))
Inputs may be any that keep to these rules, and one draw needn't show every extreme that they name: cell_map[i, j] = r * 512 + c with r within 1 of (i % 64) // 4 and 0 <= r < 16, and c within 3 of j // 4.
All inputs are finite; a program needn't handle non-finite values. No bound on the sum of `wet_mask` on one device may be relied on, other than what follows from the above.
Results may differ from a plain program's by a relative error of at most 0.0003.
Values sent between devices are 32-bit elements; how exact they have to be, the bound alone decides.
A program may use at most 64 MiB of HBM per device.

v0:
```python
import jax
import jax.numpy as jnp
from jax import lax
from jax.sharding import PartitionSpec as P

FRACTIONS = 4
SUBSTEPS = 4


gravity = 1.0
time_step = 0.2
depth_floor = 1.25
drag_coeff = 0.02
settle_base = 0.05
critical_base = 0.05
erode_base = 0.002
exner_factor = 400.0


def joined_along(pieces, dim):
    shape = list(pieces.shape[1:])
    shape[dim] *= pieces.shape[0]
    return jnp.moveaxis(pieces, 0, dim).reshape(shape)


def copy_for_each(value, axis):
    peers = lax.axis_size(axis)
    return lax.all_to_all(
        jnp.broadcast_to(value[None], (peers, *value.shape)), axis, 0, 0, tiled=True
    )


def gather_directly(value, axis, dim):
    return joined_along(copy_for_each(value, axis), dim)


def with_halo(block, sides, width):
    for axis, dim in sides:
        count = lax.axis_size(axis)
        forward = [(i, i + 1) for i in range(count - 1)]
        backward = [(target, source) for source, target in forward]
        low = lax.ppermute(
            lax.slice_in_dim(block, block.shape[dim] - width, None, axis=dim), axis, forward
        )
        high = lax.ppermute(lax.slice_in_dim(block, 0, width, axis=dim), axis, backward)
        block = jnp.concatenate([low, block, high], axis=dim)
    return block


def in_blocks(value, dim, peers):
    shape = value.shape
    pieces = value.reshape(*shape[:dim], peers, shape[dim] // peers, *shape[dim + 1 :])
    return jnp.moveaxis(pieces, dim, 0)


def sent_and_summed(value, axis, dim):
    peers = lax.axis_size(axis)
    pieces = lax.all_to_all(in_blocks(value, dim, peers), axis, 0, 0, tiled=True)
    return jnp.sum(pieces, axis=0)


def minmod(lower_diff, upper_diff):
    return (
        0.5
        * (jnp.sign(lower_diff) + jnp.sign(upper_diff))
        * jnp.minimum(jnp.abs(lower_diff), jnp.abs(upper_diff))
    )


def physical(fields, normal):
    depths = fields[0]
    speed = fields[normal] / jnp.maximum(depths, depth_floor)
    fluxes = fields * speed[None]
    fluxes = fluxes.at[normal].add(0.5 * gravity * depths * depths)
    celerity = jnp.abs(speed) + jnp.sqrt(gravity * depths)
    return (fluxes, celerity)


def face_flux(left_state, right_state, normal):
    left_flux, left_wave = physical(left_state, normal)
    right_flux, right_wave = physical(right_state, normal)
    fastest = jnp.maximum(left_wave, right_wave)
    return 0.5 * (left_flux + right_flux) - 0.5 * fastest[None] * (right_state - left_state)


def advance(fields, bed_pad, wet_pad, params):
    center = fields[:, 2:-2, 2:-2]
    along_rows = fields[:, :, 2:-2]
    slopes = minmod(
        along_rows[:, 1:-1] - along_rows[:, :-2], along_rows[:, 2:] - along_rows[:, 1:-1]
    )
    middle = along_rows[:, 1:-1]
    left_state = (middle + 0.5 * slopes)[:, :-1]
    right_state = (middle - 0.5 * slopes)[:, 1:]
    open_x = wet_pad[1:-2, 2:-2] * wet_pad[2:-1, 2:-2]
    fluxes = face_flux(left_state, right_state, 1) * open_x[None]
    net_x = fluxes[:, 1:] - fluxes[:, :-1]
    along_cols = fields[:, 2:-2, :]
    slopes = minmod(
        along_cols[:, :, 1:-1] - along_cols[:, :, :-2],
        along_cols[:, :, 2:] - along_cols[:, :, 1:-1],
    )
    middle = along_cols[:, :, 1:-1]
    left_state = (middle + 0.5 * slopes)[:, :, :-1]
    right_state = (middle - 0.5 * slopes)[:, :, 1:]
    open_y = wet_pad[2:-2, 1:-2] * wet_pad[2:-2, 2:-1]
    fluxes = face_flux(left_state, right_state, 2) * open_y[None]
    net_y = fluxes[:, :, 1:] - fluxes[:, :, :-1]
    depths = center[0]
    floored = jnp.maximum(depths, depth_floor)
    along_x = center[1] / floored
    along_y = center[2] / floored
    velocity_mag = jnp.sqrt(along_x * along_x + along_y * along_y + 1e-06)
    bed_x = 0.5 * (bed_pad[3:-1, 2:-2] - bed_pad[1:-3, 2:-2])
    bed_y = 0.5 * (bed_pad[2:-2, 3:-1] - bed_pad[2:-2, 1:-3])
    source_x = -gravity * depths * bed_x - drag_coeff * velocity_mag * along_x
    source_y = -gravity * depths * bed_y - drag_coeff * velocity_mag * along_y
    settling = settle_base * params[0][:, None, None] * center[3:] / floored[None]
    critical = critical_base * params[1][:, None, None]
    erosion = (
        erode_base
        * params[2][:, None, None]
        * jnp.maximum((velocity_mag * velocity_mag)[None] / critical - 1.0, 0.0)
    )
    exchange = settling - erosion
    sources = jnp.concatenate(
        [jnp.zeros_like(depths)[None], source_x[None], source_y[None], -exchange], axis=0
    )
    wet_center = wet_pad[2:-2, 2:-2][None]
    updated = center + time_step * wet_center * (sources - net_x - net_y)
    return (updated, time_step * wet_center * exchange)


def gather_band(strip):
    return gather_directly(strip, "col", 0)


def band_frame(band, coarse_start, tile_rows, tile_cols):
    padded = jnp.pad(band, ((1, 1), (3, 3)))
    return lax.dynamic_slice(
        padded, (jnp.int32(0), coarse_start), (tile_rows // 4 + 2, tile_cols // 4 + 6)
    )


def split_map(cell_map, band_cols, coarse_start):
    tile_rows, tile_cols = cell_map.shape
    local_rows = jnp.arange(tile_rows, dtype=jnp.int32)[:, None] // 4
    local_cols = coarse_start + jnp.arange(tile_cols, dtype=jnp.int32)[None, :] // 4
    return (cell_map // band_cols - local_rows, cell_map % band_cols - local_cols)


def window_sums(exchanged, row_offset, col_offset):
    fraction_count, tile_rows, tile_cols = exchanged.shape
    coarse_rows, coarse_cols = (tile_rows // 4, tile_cols // 4)
    shifts = jnp.arange(-3, 4, dtype=jnp.int32)
    col_hits = col_offset[None] == shifts[:, None, None]
    total = jnp.zeros((fraction_count, coarse_rows + 2, coarse_cols + 6), jnp.float32)
    for row_shift in (-1, 0, 1):
        hits = jnp.logical_and(col_hits, (row_offset == row_shift)[None])
        weighted = jnp.where(hits[:, None], exchanged[None], 0.0)
        blocks = weighted.reshape(7, fraction_count, coarse_rows, 4, coarse_cols, 4).sum(
            axis=(3, 5)
        )
        for position in range(7):
            total = total + jnp.pad(
                blocks[position], ((0, 0), (row_shift + 1, 1 - row_shift), (position, 6 - position))
            )
    return total


def window_lookup(window, row_offset, col_offset):
    tile_rows, tile_cols = row_offset.shape
    coarse_rows, coarse_cols = (tile_rows // 4, tile_cols // 4)
    result = jnp.zeros((tile_rows, tile_cols), jnp.float32)
    for row_shift in (-1, 0, 1):
        for col_shift in range(-3, 4):
            piece = window[
                row_shift + 1 : row_shift + 1 + coarse_rows,
                col_shift + 3 : col_shift + 3 + coarse_cols,
            ]
            spread = jnp.broadcast_to(
                piece[:, None, :, None], (coarse_rows, 4, coarse_cols, 4)
            ).reshape(tile_rows, tile_cols)
            chosen = jnp.logical_and(row_offset == row_shift, col_offset == col_shift)
            result = jnp.where(chosen, spread, result)
    return result


def band_from_window(total, coarse_start, band_cols):
    core = total[:, 1:-1]
    wide = jnp.zeros((core.shape[0], core.shape[1], band_cols + 6), jnp.float32)
    wide = lax.dynamic_update_slice(wide, core, (jnp.int32(0), jnp.int32(0), coarse_start))
    return wide[:, :, 3:-3]


def crop_plane(plane, margin_cut):
    return plane[margin_cut : plane.shape[0] - margin_cut, margin_cut : plane.shape[1] - margin_cut]


def local(water_depth, discharge, sediment, bed_level, cell_map, wet_mask, sediment_params):
    tile_rows, tile_cols = water_depth.shape
    band_cols = bed_level.shape[1]
    coarse_start = lax.axis_index("col") * (tile_cols // 4)
    row_offset, col_offset = split_map(cell_map, band_cols, coarse_start)
    bed_band = gather_band(bed_level)
    bed_frame = band_frame(bed_band, coarse_start, tile_rows, tile_cols)
    bed_start = window_lookup(bed_frame, row_offset, col_offset)
    wet = wet_mask.astype(jnp.float32)
    fields = jnp.concatenate([water_depth[None], discharge, sediment], axis=0)
    exchanged = jnp.zeros((FRACTIONS, tile_rows, tile_cols), jnp.float32)
    rim_width = 2 * SUBSTEPS
    bed_pad, wet_pad = (
        with_halo(bed_start, (("row", 0), ("col", 1)), rim_width),
        with_halo(wet, (("row", 0), ("col", 1)), rim_width),
    )
    padded = with_halo(fields, (("row", 1), ("col", 2)), rim_width)
    for substep in range(SUBSTEPS):
        margin_cut = 2 * substep
        padded, change = advance(
            padded,
            crop_plane(bed_pad, margin_cut),
            crop_plane(wet_pad, margin_cut),
            sediment_params,
        )
        margin = rim_width - 2 * (substep + 1)
        exchanged = exchanged + change[:, margin : margin + tile_rows, margin : margin + tile_cols]
    fields = padded
    window_total = window_sums(exchanged, row_offset, col_offset)
    local_sums = band_from_window(window_total, coarse_start, band_cols)
    strip_total = sent_and_summed(local_sums, "col", 1)
    deposit = exner_factor / 16.0 * strip_total
    bed_new = bed_level + jnp.sum(deposit, axis=0)
    band_new = gather_band(bed_new)
    fine_frame = band_frame(band_new, coarse_start, tile_rows, tile_cols)
    fine_bed = window_lookup(fine_frame, row_offset, col_offset)
    return (fields[0], fields[1:3], fields[3:], fine_bed, bed_new, deposit)


def solution(mesh):
    placed = (
        P("row", "col"),
        P(None, "row", "col"),
        P(None, "row", "col"),
        P(("row", "col"), None),
        P("row", "col"),
        P("row", "col"),
        P(),
    )
    return jax.shard_map(
        local,
        mesh=mesh,
        in_specs=placed,
        out_specs=(
            P("row", "col"),
            P(None, "row", "col"),
            P(None, "row", "col"),
            P("row", "col"),
            P(("row", "col"), None),
            P(None, ("row", "col"), None),
        ),
        check_vma=False,
    )
```

profile of v0, /device:TPU:57, one launch (start us, length us, event | category | flops | bytes accessed | tf_op | source)
XLA Modules:
  0.0 251.7 jit_solution(5682818636929215831)
XLA Ops:
  1.5 2.4 collective-permute-start.1
  3.9 5.0 %collective-permute-start = (f32[7,8,128]{2,1,0:T(8,128)S(1)}, f32[7,8,128]{2,1,0:T(8,128)S(1)}, u32[]{:S(2)}, u32[]{:S(2)}) collective-permute-start(f32[7,8,128]{2,1,0:T(8,128)S(1)} %get-tuple-element.315), channel_id=1, source_target_pairs={{0,16},{16,32},{32,48},{48,64},{64,80},{80,96},{96,112},{112,128},... | collective-permute-start | bytes 86024 | tf_op jit(solution)/shard_map/ppermute | solution.py:42
  9.6 1.9 collective-permute-start.5
  11.6 5.5 %collective-permute-start.4 = (f32[8,128]{1,0:T(8,128)S(1)}, f32[8,128]{1,0:T(8,128)S(1)}, u32[]{:S(2)}, u32[]{:S(2)}) collective-permute-start(f32[8,128]{1,0:T(8,128)S(1)} %get-tuple-element.372), channel_id=1, source_target_pairs={{0,16},{16,32},{32,48},{48,64},{64,80},{80,96},{96,112},{112,128},... | collective-permute-start | bytes 12296 | tf_op jit(solution)/shard_map/ppermute | solution.py:42
  17.0 1.3 broadcast_in_dim.147
  18.4 18.5 %all-to-all-start = ((f32[16,1,512]{2,1,0:T(1,128)}), f32[16,1,512]{2,1,0:T(1,128)S(1)}, u32[]{:S(2)}, u32[]{:S(2)}) async-start(f32[16,1,512]{2,1,0:T(1,128)} %broadcast_in_dim.147), calls=%async_computation | async-start | bytes 65536 | tf_op jit(solution)/shard_map/all_to_all | solution.py:28
  37.4 1.4 broadcast_multiply_fusion
  38.8 1.4 multiply_bitcast_fusion.14
  44.4 2.0 collective-permute-start.7
  46.4 3.5 %collective-permute-start.6 = (f32[80,8]{1,0:T(8,128)S(1)}, f32[80,8]{1,0:T(8,128)S(1)}, u32[]{:S(2)}, u32[]{:S(2)}) collective-permute-start(f32[80,8]{1,0:T(8,128)S(1)} %get-tuple-element.322), channel_id=1, source_target_pairs={{0,1},{1,2},{2,3},{3,4},{4,5},{5,6},{6,7},{7,8},{8,9},{9,10},{10,1... | collective-permute-start | bytes 7688 | tf_op jit(solution)/shard_map/ppermute | solution.py:42
  54.9 1.9 collective-permute-start.3
  56.8 4.4 %collective-permute-start.2 = (f32[7,80,8]{2,1,0:T(8,128)S(1)}, f32[7,80,8]{2,1,0:T(8,128)S(1)}, u32[]{:S(2)}, u32[]{:S(2)}) collective-permute-start(f32[7,80,8]{2,1,0:T(8,128)S(1)} %get-tuple-element.289), channel_id=1, source_target_pairs={{0,1},{1,2},{2,3},{3,4},{4,5},{5,6},{6,7},{7,8},{8,9},{9,10},{10,1... | collective-permute-start | bytes 53768 | tf_op jit(solution)/shard_map/ppermute | solution.py:42
  79.3 1.3 reshape.838
  80.8 1.3 reshape.839
  82.2 1.3 reshape.840
  85.1 1.3 reshape.842
  90.9 1.3 reshape.846
  92.1 1.8 select_select_fusion.1
  94.0 1.9 collective-permute-start.9
  95.9 5.5 %collective-permute-start.8 = (f32[8,128]{1,0:T(8,128)S(1)}, f32[8,128]{1,0:T(8,128)S(1)}, u32[]{:S(2)}, u32[]{:S(2)}) collective-permute-start(f32[8,128]{1,0:T(8,128)S(1)} %get-tuple-element.344), channel_id=1, source_target_pairs={{0,16},{16,32},{32,48},{48,64},{64,80},{80,96},{96,112},{112,128},... | collective-permute-start | bytes 12296 | tf_op jit(solution)/shard_map/ppermute | solution.py:42
  107.6 1.9 collective-permute-start.11
  109.5 5.1 %collective-permute-start.10 = (f32[80,8]{1,0:T(8,128)S(1)}, f32[80,8]{1,0:T(8,128)S(1)}, u32[]{:S(2)}, u32[]{:S(2)}) collective-permute-start(f32[80,8]{1,0:T(8,128)S(1)} %get-tuple-element.320), channel_id=1, source_target_pairs={{0,1},{1,2},{2,3},{3,4},{4,5},{5,6},{6,7},{7,8},{8,9},{9,10},{10,1... | collective-permute-start | bytes 7688 | tf_op jit(solution)/shard_map/ppermute | solution.py:42
  114.7 1.9 compare_and_fusion
  128.0 5.7 %broadcast_in_dim.186 = f32[4,16,4,32,4]{4,3,2,1,0:T(8,128)} reshape(f32[4,64,128]{2,1,0:T(8,128)S(1)} %get-tuple-element.240) | data formatting | bytes 262144 | tf_op jit(solution)/shard_map/jit(_where)/broadcast_in_dim | solution.py:160
  133.7 3.4 %copy.15 = f32[4,16,4,32,4]{3,1,4,2,0:T(8,128)S(1)} copy(f32[4,16,4,32,4]{4,3,2,1,0:T(8,128)} %broadcast_in_dim.186) | data formatting | bytes 262144 | tf_op jit(solution)/shard_map/jit(_where)/broadcast_in_dim | solution.py:160
  137.1 3.3 %select_reduce_fusion.2 = (f32[7,4,16,32]{3,2,1,0:T(8,128)S(1)}, f32[7,4,16,32]{3,2,1,0:T(8,128)S(1)}, f32[7,4,16,32]{3,2,1,0:T(8,128)S(1)}) fusion(f32[4,16,4,32,4]{3,1,4,2,0:T(8,128)S(1)} %copy.15, pred[7,16,4,32,4]{3,1,4,2,0:T(8,128)(4,1)} %get-tuple-element.319, pred[7,16,4,32,4]{3,1,4,2,0:T(8,128)(4,1)} %get-tuple-element.318, ...), kind=kLoop, calls=%fused_computation.2 | loop fusion | flops 1333248 | bytes 475136 | tf_op jit(solution)/shard_map/reduce_sum | solution.py:161
  141.0 2.5 dynamic_update_slice.3
  144.3 50.3 %all-to-all-start.1 = ((f32[16,4,1,512]{3,1,2,0:T(4,128)}), f32[16,4,1,512]{3,1,2,0:T(4,128)S(1)}, u32[]{:S(2)}, u32[]{:S(2)}) async-start(f32[16,4,1,512]{3,1,2,0:T(4,128)} %slice_bitcast_fusion), calls=%async_computation.1 | async-start | bytes 262144 | tf_op jit(solution)/shard_map/all_to_all | solution.py:58
  194.7 1.5 multiply_bitcast_fusion.10
  199.9 12.2 %all-to-all-done.1 = f32[16,4,1,512]{3,1,2,0:T(4,128)S(1)} async-done(((f32[16,4,1,512]{3,1,2,0:T(4,128)}), f32[16,4,1,512]{3,1,2,0:T(4,128)S(1)}, u32[]{:S(2)}, u32[]{:S(2)}) %all-to-all-start.1) | async-done | bytes 131104 | tf_op jit(solution)/shard_map/all_to_all | solution.py:58
  213.5 4.0 %all-to-all-start.2 = ((f32[16,1,512]{2,1,0:T(1,128)}), f32[16,1,512]{2,1,0:T(1,128)S(1)}, u32[]{:S(2)}, u32[]{:S(2)}) async-start(f32[16,1,512]{2,1,0:T(1,128)} %broadcast_in_dim.192), calls=%async_computation.2 | async-start | bytes 65536 | tf_op jit(solution)/shard_map/all_to_all | solution.py:28
  218.8 13.2 %all-to-all-done.2 = f32[16,1,512]{2,1,0:T(1,128)S(1)} async-done(((f32[16,1,512]{2,1,0:T(1,128)}), f32[16,1,512]{2,1,0:T(1,128)S(1)}, u32[]{:S(2)}, u32[]{:S(2)}) %all-to-all-start.2) | async-done | bytes 32800 | tf_op jit(solution)/shard_map/all_to_all | solution.py:28
  (331 shorter events, 79.3 us)
Async XLA Ops:
  0.6 54.0 %copy-start = (f32[4,64,128]{2,1,0:T(8,128)S(1)}, f32[4,64,128]{2,1,0:T(8,128)}, u32[]{:S(2)}) copy-start(f32[4,64,128]{2,1,0:T(8,128)} %param.41) | copy-start | bytes 393220
  0.6 54.0 %copy-start.1 = (f32[2,64,128]{2,1,0:T(8,128)S(1)}, f32[2,64,128]{2,1,0:T(8,128)}, u32[]{:S(2)}) copy-start(f32[2,64,128]{2,1,0:T(8,128)} %param.40) | copy-start | bytes 196612
  0.7 54.0 %copy-start.8 = (f32[64,128]{1,0:T(8,128)S(1)}, f32[64,128]{1,0:T(8,128)}, u32[]{:S(2)}) copy-start(f32[64,128]{1,0:T(8,128)} %param.39) | copy-start | bytes 98308
  1.5 53.2 %collective-permute-start.1 = (f32[7,8,128]{2,1,0:T(8,128)S(1)}, f32[7,8,128]{2,1,0:T(8,128)S(1)}, u32[]{:S(2)}, u32[]{:S(2)}) collective-permute-start(f32[7,8,128]{2,1,0:T(8,128)S(1)} %get-tuple-element.316), channel_id=1, source_target_pairs={{16,0},{32,16},{48,32},{64,48},{80,64},{96,80},{112,96},{128,112},... | collective-permute-start | bytes 86024 | tf_op jit(solution)/shard_map/ppermute | solution.py:45
  3.9 50.8 %collective-permute-start = (f32[7,8,128]{2,1,0:T(8,128)S(1)}, f32[7,8,128]{2,1,0:T(8,128)S(1)}, u32[]{:S(2)}, u32[]{:S(2)}) collective-permute-start(f32[7,8,128]{2,1,0:T(8,128)S(1)} %get-tuple-element.315), channel_id=1, source_target_pairs={{0,16},{16,32},{32,48},{48,64},{64,80},{80,96},{96,112},{112,128},... | collective-permute-start | bytes 86024 | tf_op jit(solution)/shard_map/ppermute | solution.py:42
  9.6 34.7 %collective-permute-start.5 = (f32[8,128]{1,0:T(8,128)S(1)}, f32[8,128]{1,0:T(8,128)S(1)}, u32[]{:S(2)}, u32[]{:S(2)}) collective-permute-start(f32[8,128]{1,0:T(8,128)S(1)} %get-tuple-element.373), channel_id=1, source_target_pairs={{16,0},{32,16},{48,32},{64,48},{80,64},{96,80},{112,96},{128,112},... | collective-permute-start | bytes 12296 | tf_op jit(solution)/shard_map/ppermute | solution.py:45
  11.6 32.8 %collective-permute-start.4 = (f32[8,128]{1,0:T(8,128)S(1)}, f32[8,128]{1,0:T(8,128)S(1)}, u32[]{:S(2)}, u32[]{:S(2)}) collective-permute-start(f32[8,128]{1,0:T(8,128)S(1)} %get-tuple-element.372), channel_id=1, source_target_pairs={{0,16},{16,32},{32,48},{48,64},{64,80},{80,96},{96,112},{112,128},... | collective-permute-start | bytes 12296 | tf_op jit(solution)/shard_map/ppermute | solution.py:42
  18.4 49.8 %all-to-all-start = ((f32[16,1,512]{2,1,0:T(1,128)}), f32[16,1,512]{2,1,0:T(1,128)S(1)}, u32[]{:S(2)}, u32[]{:S(2)}) async-start(f32[16,1,512]{2,1,0:T(1,128)} %broadcast_in_dim.147), calls=%async_computation | async-start | bytes 65536 | tf_op jit(solution)/shard_map/all_to_all | solution.py:28
  44.4 6.2 %collective-permute-start.7 = (f32[80,8]{1,0:T(8,128)S(1)}, f32[80,8]{1,0:T(8,128)S(1)}, u32[]{:S(2)}, u32[]{:S(2)}) collective-permute-start(f32[80,8]{1,0:T(8,128)S(1)} %get-tuple-element.323), channel_id=1, source_target_pairs={{1,0},{2,1},{3,2},{4,3},{5,4},{6,5},{7,6},{8,7},{9,8},{10,9},{11,1... | collective-permute-start | bytes 7688 | tf_op jit(solution)/shard_map/ppermute | solution.py:45
  46.4 4.6 %collective-permute-start.6 = (f32[80,8]{1,0:T(8,128)S(1)}, f32[80,8]{1,0:T(8,128)S(1)}, u32[]{:S(2)}, u32[]{:S(2)}) collective-permute-start(f32[80,8]{1,0:T(8,128)S(1)} %get-tuple-element.322), channel_id=1, source_target_pairs={{0,1},{1,2},{2,3},{3,4},{4,5},{5,6},{6,7},{7,8},{8,9},{9,10},{10,1... | collective-permute-start | bytes 7688 | tf_op jit(solution)/shard_map/ppermute | solution.py:42
  53.1 13.1 %copy-start.2 = (f32[72,136]{1,0:T(8,128)}, f32[72,136]{1,0:T(8,128)S(1)}, u32[]{:S(2)}) copy-start(f32[72,136]{1,0:T(8,128)S(1)} %slice_multiply_fusion.32) | copy-start | bytes 117508
  54.9 9.1 %collective-permute-start.3 = (f32[7,80,8]{2,1,0:T(8,128)S(1)}, f32[7,80,8]{2,1,0:T(8,128)S(1)}, u32[]{:S(2)}, u32[]{:S(2)}) collective-permute-start(f32[7,80,8]{2,1,0:T(8,128)S(1)} %get-tuple-element.290), channel_id=1, source_target_pairs={{1,0},{2,1},{3,2},{4,3},{5,4},{6,5},{7,6},{8,7},{9,8},{10,9},{11,1... | collective-permute-start | bytes 53768 | tf_op jit(solution)/shard_map/ppermute | solution.py:45
  56.8 7.8 %collective-permute-start.2 = (f32[7,80,8]{2,1,0:T(8,128)S(1)}, f32[7,80,8]{2,1,0:T(8,128)S(1)}, u32[]{:S(2)}, u32[]{:S(2)}) collective-permute-start(f32[7,80,8]{2,1,0:T(8,128)S(1)} %get-tuple-element.289), channel_id=1, source_target_pairs={{0,1},{1,2},{2,3},{3,4},{4,5},{5,6},{6,7},{7,8},{8,9},{9,10},{10,1... | collective-permute-start | bytes 53768 | tf_op jit(solution)/shard_map/ppermute | solution.py:42
  86.5 5.6 %copy-start.17 = (s32[64,128]{1,0:T(8,128)S(1)}, s32[64,128]{1,0:T(8,128)}, u32[]{:S(2)}) copy-start(s32[64,128]{1,0:T(8,128)} %param.43) | copy-start | bytes 98308
  86.6 5.6 %copy-start.46 = (pred[64,128]{1,0:T(8,128)(4,1)S(1)}, pred[64,128]{1,0:T(8,128)(4,1)}, u32[]{:S(2)}) copy-start(pred[64,128]{1,0:T(8,128)(4,1)} %get-tuple-element.349) | copy-start | bytes 24580
  92.1 25.4 %copy-start.51 = (f32[7]{0:T(128)S(1)}, f32[7]{0:T(128)}, u32[]{:S(2)}) copy-start(f32[7]{0:T(128)} %pad.182.clone) | copy-start | bytes 88
  94.0 13.5 %collective-permute-start.9 = (f32[8,128]{1,0:T(8,128)S(1)}, f32[8,128]{1,0:T(8,128)S(1)}, u32[]{:S(2)}, u32[]{:S(2)}) collective-permute-start(f32[8,128]{1,0:T(8,128)S(1)} %get-tuple-element.345), channel_id=1, source_target_pairs={{16,0},{32,16},{48,32},{64,48},{80,64},{96,80},{112,96},{128,112},... | collective-permute-start | bytes 12296 | tf_op jit(solution)/shard_map/ppermute | solution.py:45
  95.9 11.6 %collective-permute-start.8 = (f32[8,128]{1,0:T(8,128)S(1)}, f32[8,128]{1,0:T(8,128)S(1)}, u32[]{:S(2)}, u32[]{:S(2)}) collective-permute-start(f32[8,128]{1,0:T(8,128)S(1)} %get-tuple-element.344), channel_id=1, source_target_pairs={{0,16},{16,32},{32,48},{48,64},{64,80},{80,96},{96,112},{112,128},... | collective-permute-start | bytes 12296 | tf_op jit(solution)/shard_map/ppermute | solution.py:42
  107.5 11.0 %copy-start.21 = (f32[8,128]{1,0:T(8,128)}, f32[8,128]{1,0:T(8,128)S(1)}, u32[]{:S(2)}) copy-start(f32[8,128]{1,0:T(8,128)S(1)} %collective-permute-done.9) | copy-start | bytes 12292
  107.5 11.0 %copy-start.23 = (f32[8,128]{1,0:T(8,128)}, f32[8,128]{1,0:T(8,128)S(1)}, u32[]{:S(2)}) copy-start(f32[8,128]{1,0:T(8,128)S(1)} %collective-permute-done.8) | copy-start | bytes 12292
  107.6 9.0 %collective-permute-start.11 = (f32[80,8]{1,0:T(8,128)S(1)}, f32[80,8]{1,0:T(8,128)S(1)}, u32[]{:S(2)}, u32[]{:S(2)}) collective-permute-start(f32[80,8]{1,0:T(8,128)S(1)} %get-tuple-element.321), channel_id=1, source_target_pairs={{1,0},{2,1},{3,2},{4,3},{5,4},{6,5},{7,6},{8,7},{9,8},{10,9},{11,1... | collective-permute-start | bytes 7688 | tf_op jit(solution)/shard_map/ppermute | solution.py:45
  109.5 7.1 %collective-permute-start.10 = (f32[80,8]{1,0:T(8,128)S(1)}, f32[80,8]{1,0:T(8,128)S(1)}, u32[]{:S(2)}, u32[]{:S(2)}) collective-permute-start(f32[80,8]{1,0:T(8,128)S(1)} %get-tuple-element.320), channel_id=1, source_target_pairs={{0,1},{1,2},{2,3},{3,4},{4,5},{5,6},{6,7},{7,8},{8,9},{9,10},{10,1... | collective-permute-start | bytes 7688 | tf_op jit(solution)/shard_map/ppermute | solution.py:42
  140.4 55.7 %copy-start.11 = (f32[64,129]{1,0:T(8,128)S(1)}, f32[64,129]{1,0:T(8,128)}, u32[]{:S(2)}) copy-start(f32[64,129]{1,0:T(8,128)} %fusion.115) | copy-start | bytes 99076
  140.4 55.9 %copy-start.13 = (f32[80,8]{1,0:T(8,128)S(1)}, f32[80,8]{1,0:T(8,128)}, u32[]{:S(2)}) copy-start(f32[80,8]{1,0:T(8,128)} %copy-done.12) | copy-start | bytes 7684
  140.4 55.9 %copy-start.15 = (f32[80,8]{1,0:T(8,128)S(1)}, f32[80,8]{1,0:T(8,128)}, u32[]{:S(2)}) copy-start(f32[80,8]{1,0:T(8,128)} %copy-done.14) | copy-start | bytes 7684
  140.5 55.9 %copy-start.22 = (f32[8,128]{1,0:T(8,128)S(1)}, f32[8,128]{1,0:T(8,128)}, u32[]{:S(2)}) copy-start(f32[8,128]{1,0:T(8,128)} %copy-done.21) | copy-start | bytes 12292
  140.5 55.9 %copy-start.24 = (f32[8,128]{1,0:T(8,128)S(1)}, f32[8,128]{1,0:T(8,128)}, u32[]{:S(2)}) copy-start(f32[8,128]{1,0:T(8,128)} %copy-done.23) | copy-start | bytes 12292
  140.5 56.1 %copy-start.16 = (f32[65,128]{1,0:T(8,128)S(1)}, f32[65,128]{1,0:T(8,128)}, u32[]{:S(2)}) copy-start(f32[65,128]{1,0:T(8,128)} %fusion.123) | copy-start | bytes 99844
  140.5 57.2 %copy-start.10 = (f32[64,128]{1,0:T(8,128)S(1)}, f32[64,128]{1,0:T(8,128)}, u32[]{:S(2)}) copy-start(f32[64,128]{1,0:T(8,128)} %broadcast_multiply_fusion) | copy-start | bytes 98308
  144.3 67.8 %all-to-all-start.1 = ((f32[16,4,1,512]{3,1,2,0:T(4,128)}), f32[16,4,1,512]{3,1,2,0:T(4,128)S(1)}, u32[]{:S(2)}, u32[]{:S(2)}) async-start(f32[16,4,1,512]{3,1,2,0:T(4,128)} %slice_bitcast_fusion), calls=%async_computation.1 | async-start | bytes 262144 | tf_op jit(solution)/shard_map/all_to_all | solution.py:58
  212.9 22.2 %copy-start.50 = (f32[1,512]{1,0:T(1,128)}, f32[1,512]{1,0:T(1,128)S(1)}, u32[]{:S(2)}) copy-start(f32[1,512]{1,0:T(1,128)S(1)} %add.604) | copy-start | bytes 6148
  213.5 18.4 %all-to-all-start.2 = ((f32[16,1,512]{2,1,0:T(1,128)}), f32[16,1,512]{2,1,0:T(1,128)S(1)}, u32[]{:S(2)}, u32[]{:S(2)}) async-start(f32[16,1,512]{2,1,0:T(1,128)} %broadcast_in_dim.192), calls=%async_computation.2 | async-start | bytes 65536 | tf_op jit(solution)/shard_map/all_to_all | solution.py:28
  (35 other events, 91.3 us)
where the time goes:
time: 256 us; the launch traced here: 252 us
  starting transfers between devices  114 us (45%)
  local copies, waits for them, and re-layouts  69.3 us (27%)
  other arithmetic  39.4 us (15%)
  waiting for transfers between devices  26.5 us (10%)
  between operations  2.7 us (1%)
    all_to_all x1, starting transfers between devices, sent_and_summed(): lax.all_to_all(in_blocks(value, dim, peers), axis, 0, 0, tiled=True)  50.3 us
    reshape x42, local copies, waits for them, and re-layouts, window_lookup(): spread = jnp.broadcast_to(piece[:, None, :, None], (coarse_rows, 4, coars...  33.3 us
    ppermute x6, starting transfers between devices, with_halo(): lax.ppermute(lax.slice_in_dim(block, block.shape[dim] - width, None, axis...  29 us
    all_to_all x2, starting transfers between devices, copy_for_each(): lax.all_to_all(jnp.broadcast_to(value[None], (peers, *value.shape)), axis...  22.5 us
    all_to_all x2, waiting for transfers between devices, copy_for_each(): lax.all_to_all(jnp.broadcast_to(value[None], (peers, *value.shape)), axis...  13.2 us
    all_to_all x1, waiting for transfers between devices, sent_and_summed(): lax.all_to_all(in_blocks(value, dim, peers), axis, 0, 0, tiled=True)  12.2 us
    ppermute x6, starting transfers between devices, with_halo(): lax.ppermute(lax.slice_in_dim(block, 0, width, axis=dim), axis, backward)  12 us
    broadcast_in_dim x2, local copies, waits for them, and re-layouts, window_sums(): weighted = jnp.where(hits[:, None], exchanged[None], 0.0)  9.06 us
  transfers between devices with their start and end apart: 15, of which 4 were waited for; matrix products, arithmetic and copies ran while one was open for 14% of the time, Pallas kernels for 0%

commit v1 on v0

v1 whole, which is shorter than its diff:
```python
import jax
import jax.numpy as jnp
from jax import lax
from jax.experimental import pallas as pl
from jax.experimental.pallas import tpu as pltpu
from jax.sharding import PartitionSpec as P

FRACTIONS = 4
SUBSTEPS = 4
ROWS = 32
COLS = 16
SEG = 10

MESH = pl.DeviceIdType.MESH
f32 = jnp.float32
i32 = jnp.int32


def roll(x, shift, axis):
    return pltpu.roll(x, shift % x.shape[axis], axis)


def minmod(a, b):
    return jnp.maximum(jnp.minimum(b, 0.0), jnp.minimum(a, jnp.maximum(b, 0.0)))


def face_factors(h_l, n_l, h_r, n_r, opened):
    w_l = n_l / jnp.maximum(h_l, 2.5)
    w_r = n_r / jnp.maximum(h_r, 2.5)
    c_l = jnp.abs(w_l) + jnp.sqrt(0.5 * h_l)
    c_r = jnp.abs(w_r) + jnp.sqrt(0.5 * h_r)
    fastest = jnp.maximum(c_l, c_r)
    push = (0.25 * opened) * (h_l * h_l + h_r * h_r)
    return opened * (w_l + fastest), opened * (w_r - fastest), push


def kernel(
    depth, disch, sed, bed, cmap, wetm, par,
    o_depth, o_disch, o_sed, o_fine, o_bed, o_dep,
    nat, raw, bedv, pk, rx, strips, band, band2, cn, nbed,
    ibuf, rbuf, kbuf, fld, wet, gx, gy, ox, oy, wd, lc, fc, coef,
    exch, on, exn, sel, mhi, mlo, tot, nsum, nrx, rs, wnew, fineb, depv, bedo,
    in_sem, nb_send, nb_recv, st_send, st_recv, ph_send, ph_recv, ns_send, ns_recv, out_sem,
):
    R = lax.axis_index("row")
    C = lax.axis_index("col")
    barrier = pltpu.get_barrier_semaphore()

    def greet(c, carry):
        near = jnp.abs(c - C) <= 1

        @pl.when(c != C)
        def _():
            pl.semaphore_signal(barrier, inc=1, device_id=(R, c), device_id_type=MESH)

        @pl.when(jnp.logical_and(R > 0, jnp.logical_or(near, c >= COLS - 3)))
        def _():
            pl.semaphore_signal(barrier, inc=1, device_id=(R - 1, c), device_id_type=MESH)

        @pl.when(jnp.logical_and(R < ROWS - 1, jnp.logical_or(near, c <= 2)))
        def _():
            pl.semaphore_signal(barrier, inc=1, device_id=(R + 1, c), device_id_type=MESH)

        return carry

    lax.fori_loop(0, COLS, greet, 0)

    mid = pl.ds(8, 64)
    loads = [
        pltpu.make_async_copy(depth, nat.at[0, mid], in_sem.at[0]),
        pltpu.make_async_copy(disch, nat.at[pl.ds(1, 2), mid], in_sem.at[1]),
        pltpu.make_async_copy(sed, nat.at[pl.ds(3, 4), mid], in_sem.at[2]),
        pltpu.make_async_copy(bed, bedv, in_sem.at[3]),
        pltpu.make_async_copy(cmap, raw.at[0], in_sem.at[4]),
        pltpu.make_async_copy(wetm, raw.at[1], in_sem.at[5]),
    ]
    for copy in loads:
        copy.start()

    lane = lax.broadcasted_iota(i32, (8, 128), 1)
    sub = lax.broadcasted_iota(i32, (8, 128), 0)
    masks = [((lane + 8 - 16 * q) & 127) < 16 for q in range(8)]

    far = f32(1 << 20)

    @pl.when(R == 0)
    def _():
        nat[0:8, 0:8, :] = jnp.zeros((8, 8, 128), f32)
        nat[8, 0:8, :] = jnp.full((8, 128), far)
        band[0:3] = jnp.zeros((3, 1, 128), f32)

    @pl.when(R == ROWS - 1)
    def _():
        nat[0:8, 72:80, :] = jnp.zeros((8, 8, 128), f32)
        nat[8, 72:80, :] = jnp.full((8, 128), far)
        band[19:22] = jnp.zeros((3, 1, 128), f32)

    for side, edge in ((0, C == COLS - 1), (1, C == 0)):

        @pl.when(edge)
        def _(side=side):
            rx[side, 0] = jnp.full((8, 128), far)
            rx[side, 1:9] = jnp.zeros((8, 8, 128), f32)

        @pl.when(jnp.logical_or(edge, R == 0))
        def _(side=side):
            rx[side, 9] = jnp.zeros((8, 128), f32)
            rx[side, 10] = jnp.full((8, 128), far)

        @pl.when(jnp.logical_or(edge, R == ROWS - 1))
        def _(side=side):
            rx[side, 11] = jnp.full((8, 128), far)
            rx[side, 12] = jnp.zeros((8, 128), f32)

    @pl.when(C == COLS - 1)
    def _():
        nrx[0] = jnp.zeros((16, 128), f32)

    @pl.when(C == 0)
    def _():
        nrx[1] = jnp.zeros((16, 128), f32)

    tot[...] = jnp.zeros((128, 128), f32)
    wnew[...] = jnp.zeros((24, 128), f32)

    from_col = lax.broadcasted_iota(i32, (128, 128), 0) // 4
    to_lane = lax.broadcasted_iota(i32, (128, 128), 1)
    for d in range(7):
        sel[128 * d : 128 * d + 128, :] = (
            jnp.where(to_lane - from_col == d + 5, 1.0, 0.0).astype(jnp.bfloat16)
        )

    for k in range(FRACTIONS):
        erode = 0.002 * jnp.full((8, 128), par[2, k], f32)
        coef[0, k] = 0.05 * jnp.full((8, 128), par[0, k], f32)
        coef[1, k] = erode / (0.05 * jnp.full((8, 128), par[1, k], f32))
        coef[2, k] = erode

    for copy in loads:
        copy.wait()
    nat[8, 8:72, :] = raw[0].astype(f32)
    nat[7, 8:72, :] = raw[1].astype(f32)

    at = 32 * lax.broadcasted_iota(i32, (16, 128), 0) - 8 + lax.broadcasted_iota(i32, (16, 128), 1)
    window = jnp.zeros((16, 128), f32)
    for q in range(4):
        chunk = jnp.broadcast_to(bedv[:, 128 * q : 128 * q + 128], (16, 128))
        got = jnp.take_along_axis(chunk, at & 127, axis=1, mode="promise_in_bounds")
        window = jnp.where((at >> 7) == q, got, window)
    for t in range(COLS):
        strips[t] = window[t : t + 1, :]

    map_pack = None
    for g in range(8):
        rows = slice(8 + 8 * g, 16 + 8 * g)
        packed = nat[0, rows, :]
        for q in range(1, 8):
            packed = jnp.where(masks[q], roll(nat[q, rows, :], 16 * q, 1), packed)
        pk[1 + g] = packed
        moved = roll(nat[8, rows, :], 16 * g, 1)
        map_pack = moved if g == 0 else jnp.where(masks[g], moved, map_pack)
    pk[0] = map_pack
    pk[9] = map_pack

    up, down = R > 0, R < ROWS - 1
    left, right = C > 0, C < COLS - 1
    both = jnp.logical_and
    above = jnp.where(C <= 2, COLS, jnp.where(C == COLS - 1, 2, 3))
    below = jnp.where(C >= COLS - 3, COLS, jnp.where(C == 0, 2, 3))
    expected = COLS - 1 + jnp.where(up, above, 0) + jnp.where(down, below, 0)
    pl.semaphore_wait(barrier, expected)

    def remote(src, dst, send, recv, device):
        return pltpu.make_async_remote_copy(
            src_ref=src, dst_ref=dst, send_sem=send, recv_sem=recv,
            device_id=device, device_id_type=MESH,
        )

    plan = [
        (left, pk.at[pl.ds(0, 9)], rx.at[0, pl.ds(0, 9)], (R, C - 1), right),
        (right, pk.at[pl.ds(0, 9)], rx.at[1, pl.ds(0, 9)], (R, C + 1), left),
        (up, nat.at[:, pl.ds(8, 8)], nat.at[:, pl.ds(72, 8)], (R - 1, C), down),
        (down, nat.at[:, pl.ds(64, 8)], nat.at[:, pl.ds(0, 8)], (R + 1, C), up),
        (both(up, left), pk.at[pl.ds(0, 2)], rx.at[0, pl.ds(11, 2)], (R - 1, C - 1), both(down, right)),
        (both(up, right), pk.at[pl.ds(0, 2)], rx.at[1, pl.ds(11, 2)], (R - 1, C + 1), both(down, left)),
        (both(down, left), pk.at[pl.ds(8, 2)], rx.at[0, pl.ds(9, 2)], (R + 1, C - 1), both(up, right)),
        (both(down, right), pk.at[pl.ds(8, 2)], rx.at[1, pl.ds(9, 2)], (R + 1, C + 1), both(up, left)),
    ]
    for n, (sends, src, dst, device, _) in enumerate(plan):

        @pl.when(sends)
        def _(n=n, src=src, dst=dst, device=device):
            remote(src, dst, nb_send.at[n], nb_recv.at[n], device).start()

    def send_strips(t, carry):
        @pl.when(t != C)
        def _():
            remote(strips.at[t], band.at[3 + C], st_send.at[0], st_recv.at[0], (R, t)).start()

        @pl.when(both(C <= 2, up))
        def _():
            remote(strips.at[t], band.at[19 + C], st_send.at[1], st_recv.at[1], (R - 1, t)).start()

        @pl.when(both(C >= COLS - 3, down))
        def _():
            remote(strips.at[t], band.at[C - 13], st_send.at[1], st_recv.at[2], (R + 1, t)).start()

        return carry

    lax.fori_loop(0, COLS, send_strips, 0)
    band[3 + C] = strips[C]

    for n, (_, src, dst, device, gets) in enumerate(plan):

        @pl.when(gets)
        def _(n=n, src=src, dst=dst, device=device):
            pltpu.make_async_copy(src, dst, nb_recv.at[n]).wait()

    lower_half = (lane & 15) < 8
    for g in range(10):
        slot = 9 if g == 0 else (12 if g == 9 else g)
        cn[8 * g : 8 * g + 8, :] = jnp.where(lower_half, rx[0, slot], rx[1, slot])
    for t in range(SEG):
        side = cn[pl.ds(t, 8, stride=SEG), :]
        for q in range(8):
            rolled = roll(side, -16 * q, 1)
            own = nat[q, pl.ds(t, 8, stride=SEG), :]
            if q < 7:
                fld[q, t + 2, :, 0:128] = own
                fld[q, t + 2, :, 128:256] = rolled
            else:
                wet[t + 1, :, 0:128] = own
                wet[t + 1, :, 128:256] = rolled
    wet[0] = roll(wet[SEG], 1, 0)
    wet[SEG + 1] = roll(wet[1], -1, 0)
    for t in range(-1, SEG):
        w = wet[t + 1]
        ox[t + 1] = 0.05 * w * wet[t + 2]
        if t >= 0:
            oy[t] = 0.05 * w * roll(w, -1, 1)
            wd[t] = 0.2 * w

    pltpu.make_async_copy(strips.at[pl.ds(0, 15)], band.at[pl.ds(3, 15)], st_recv.at[0]).wait()

    @pl.when(down)
    def _():
        pltpu.make_async_copy(strips.at[pl.ds(0, 3)], band.at[pl.ds(19, 3)], st_recv.at[1]).wait()

    @pl.when(up)
    def _():
        pltpu.make_async_copy(strips.at[pl.ds(0, 3)], band.at[pl.ds(0, 3)], st_recv.at[2]).wait()

    for e in range(22):
        band2[e : e + 1, :] = band[e]

    map_side = jnp.where(lower_half, rx[0, 0], rx[1, 0])
    map_top = jnp.where(lower_half, rx[0, 10], rx[1, 10])
    map_low = jnp.where(lower_half, rx[0, 11], rx[1, 11])
    top_half = sub < 4

    def looked_up(table, first_row, index, shift):
        rows = [jnp.broadcast_to(table[first_row + n : first_row + n + 1, :], (8, 128)) for n in range(4)]
        result = jnp.zeros((8, 128), f32)
        for n in range(3):
            pair = jnp.where(top_half, rows[n], rows[n + 1])
            got = jnp.take_along_axis(pair, index, axis=1, mode="promise_in_bounds")
            result = jnp.where(shift == n - 1, got, result)
        return result

    for g in range(10):
        rows = slice(8 * g, 8 * g + 8)
        if g == 0:
            beside = roll(map_top, -16 * 7, 1)
        elif g == 9:
            beside = map_low
        else:
            beside = roll(map_side, -16 * (g - 1), 1)
        for tile, values in enumerate((nat[8, rows, :], beside)):
            cells = values.astype(i32)
            base = 2 * g - 2 + (sub >> 2)
            shift = (cells >> 9) - base + (-16 if g == 0 else (16 if g == 9 else 0))
            index = ((cells & 511) - 32 * C + 8) & 127
            nbed[tile, rows, :] = looked_up(band2, 2 * g - 2 - 1 + 3, index, shift)
            if tile == 0:
                ibuf[rows, :] = index
                rbuf[rows, :] = shift
                kbuf[rows, :] = (shift + 1) * 7 + (index - 8 - (lane >> 2) + 3)

    def bed_plane(t):
        return jnp.concatenate(
            [nbed[0, pl.ds(t, 8, stride=SEG), :], nbed[1, pl.ds(t, 8, stride=SEG), :]], axis=1
        )

    for t in range(SEG):
        here = bed_plane(t)
        below_bed = roll(bed_plane(SEG - 1), 1, 0) if t == 0 else bed_plane(t - 1)
        above_bed = roll(bed_plane(0), -1, 0) if t == SEG - 1 else bed_plane(t + 1)
        scale = -0.5 * wd[t]
        gx[t] = scale * (above_bed - below_bed)
        gy[t] = scale * (roll(here, -1, 1) - roll(here, 1, 1))

    exch[...] = jnp.zeros(exch.shape, f32)

    def x_states(q, t):
        q0, q1, q2 = fld[q, t + 2], fld[q, t + 3], fld[q, t + 4]
        s = minmod(q1 - q0, q2 - q1)
        twice = q1 + q1
        return twice + s, twice - s

    def substep(_, carry):
        for q in range(7):
            fld[q, 0] = roll(fld[q, 10], 1, 0)
            fld[q, 1] = roll(fld[q, 11], 1, 0)
            fld[q, 12] = roll(fld[q, 2], -1, 0)
            fld[q, 13] = roll(fld[q, 3], -1, 0)
        for q in range(7):
            q0, q1, q2 = fld[q, 0], fld[q, 1], fld[q, 2]
            s = minmod(q1 - q0, q2 - q1)
            lc[q] = q1 + q1 + s

        def x_faces(t):
            lows = {}
            for q in (0, 1):
                left_new, right_new = x_states(q, t)
                lows[q] = (lc[q], left_new, right_new)
            a, b, push = face_factors(lows[0][0], lows[1][0], lows[0][2], lows[1][2], ox[t + 1])
            net = []
            for q in range(7):
                if q in lows:
                    left_old, left_new, right_new = lows[q]
                else:
                    left_new, right_new = x_states(q, t)
                    left_old = lc[q]
                lc[q] = left_new
                flux = left_old * a + right_new * b
                if q == 1:
                    flux = flux + push
                net.append((flux, q))
            return net

        for flux, q in x_faces(-1):
            fc[q] = flux

        def plane(t, inner):
            net = []
            for flux, q in x_faces(t):
                net.append(flux - fc[q])
                fc[q] = flux
            values = [fld[q, t + 2] for q in range(7)]

            def y_states(q):
                v = values[q]
                d = roll(v, -1, 1) - v
                s = minmod(roll(d, 1, 1), d)
                twice = v + v
                return twice + s, roll(twice - s, -1, 1)

            h_l, h_r = y_states(0)
            n_l, n_r = y_states(2)
            a, b, push = face_factors(h_l, n_l, h_r, n_r, oy[t])
            for q in range(7):
                if q == 0:
                    lo, hi = h_l, h_r
                elif q == 2:
                    lo, hi = n_l, n_r
                else:
                    lo, hi = y_states(q)
                flux = lo * a + hi * b
                if q == 2:
                    flux = flux + push
                net[q] = net[q] + (flux - roll(flux, 1, 1))
            h = values[0]
            inv = 1.0 / jnp.maximum(h, 1.25)
            u, v = values[1] * inv, values[2] * inv
            s2 = u * u + v * v + 1e-6
            w = wd[t]
            drag = (0.02 * w) * jnp.sqrt(s2)
            fld[0, t + 2] = h - net[0]
            fld[1, t + 2] = values[1] - net[1] + (h * gx[t] - drag * u)
            fld[2, t + 2] = values[2] - net[2] + (h * gy[t] - drag * v)
            settle = inv * w
            for k in range(FRACTIONS):
                two = lambda n: jnp.concatenate([coef[n, k], coef[n, k]], axis=1)
                m = values[3 + k]
                erosion = jnp.maximum(s2 * two(1) - two(2), 0.0)
                change = two(0) * m * settle - erosion * w
                exch[k, t] += change[:, 0:128]
                fld[3 + k, t + 2] = m - net[3 + k] - change
            return inner

        lax.fori_loop(0, SEG, plane, 0)
        return carry

    lax.fori_loop(0, SUBSTEPS, substep, 0)

    for t in range(SEG):
        for q in range(7):
            on[q, pl.ds(t, 8, stride=SEG), :] = fld[q, t + 2, :, 0:128]
        for k in range(FRACTIONS):
            exn[k, pl.ds(t, 8, stride=SEG), :] = exch[k, t]
    stores = [
        pltpu.make_async_copy(on.at[0, mid], o_depth, out_sem.at[0]),
        pltpu.make_async_copy(on.at[pl.ds(1, 2), mid], o_disch, out_sem.at[1]),
        pltpu.make_async_copy(on.at[pl.ds(3, 4), mid], o_sed, out_sem.at[2]),
    ]
    for copy in stores:
        copy.start()

    keys = [kbuf[pl.ds(8 + p, 16, stride=4), :] for p in range(4)]
    planes = [[exn[k, pl.ds(8 + p, 16, stride=4), :] for p in range(4)] for k in range(FRACTIONS)]
    for r in range(3):
        for d in range(7):
            hits = [keys[p] == r * 7 + d for p in range(4)]
            for k in range(FRACTIONS):
                acc = jnp.where(hits[0], planes[k][0], 0.0)
                for p in range(1, 4):
                    acc = acc + jnp.where(hits[p], planes[k][p], 0.0)
                high = acc.astype(jnp.bfloat16)
                rows = slice(64 * r + 16 * k, 64 * r + 16 * k + 16)
                mhi[rows, 128 * d : 128 * d + 128] = high
                mlo[rows, 128 * d : 128 * d + 128] = (acc - high.astype(f32)).astype(jnp.bfloat16)
    res = jnp.dot(mhi[...], sel[...], preferred_element_type=f32)
    res = res + jnp.dot(mlo[...], sel[...], preferred_element_type=f32)
    every = None
    for k in range(FRACTIONS):
        part = res[64 + 16 * k : 80 + 16 * k]
        part = part + roll(res[16 * k : 16 * k + 16], -1, 0)
        part = part + roll(res[128 + 16 * k : 144 + 16 * k], 1, 0)
        part = 25.0 * part
        tot[pl.ds(k, 16, stride=8), :] = part
        every = part if k == 0 else every + part
    nsum[...] = every

    @pl.when(left)
    def _():
        remote(nsum, nrx.at[0], ns_send.at[0], ns_recv.at[0], (R, C - 1)).start()

    @pl.when(right)
    def _():
        remote(nsum, nrx.at[1], ns_send.at[1], ns_recv.at[1], (R, C + 1)).start()

    def send_sums(r, carry):
        @pl.when(r != C)
        def _():
            remote(
                tot.at[pl.ds(pl.multiple_of(8 * r, 8), 8)], rs.at[pl.ds(pl.multiple_of(8 * C, 8), 8)],
                ph_send, ph_recv, (R, r),
            ).start()

        return carry

    lax.fori_loop(0, COLS, send_sums, 0)
    own_rows = pl.ds(pl.multiple_of(8 * C, 8), 8)
    rs[own_rows, :] = tot[own_rows, :]

    @pl.when(right)
    def _():
        pltpu.make_async_copy(nsum, nrx.at[0], ns_recv.at[0]).wait()

    @pl.when(left)
    def _():
        pltpu.make_async_copy(nsum, nrx.at[1], ns_recv.at[1]).wait()

    wnew[1:17, :] = band2[3:19, :] + (nsum[...] + roll(nrx[0], 32, 1) + roll(nrx[1], -32, 1))
    for g in range(8):
        rows = slice(8 + 8 * g, 16 + 8 * g)
        fineb[8 * g : 8 * g + 8, :] = looked_up(wnew, 2 * g, ibuf[rows, :], rbuf[rows, :])
    fine_store = pltpu.make_async_copy(fineb, o_fine, out_sem.at[3])
    fine_store.start()

    pltpu.make_async_copy(tot.at[pl.ds(0, 120)], rs.at[pl.ds(0, 120)], ph_recv).wait()
    chunks = [jnp.zeros((8, 128), f32) for _ in range(4)]
    low_lanes = lane < 64
    for s in range(COLS):
        q, m = divmod(s, 4)
        piece = roll(rs[8 * s : 8 * s + 8, :], 32 * m - 8, 1)
        if m == 0:
            chunks[q] = chunks[q] + jnp.where(low_lanes, piece, 0.0)
            if q > 0:
                chunks[q - 1] = chunks[q - 1] + jnp.where(low_lanes, 0.0, piece)
        elif m == 3:
            chunks[q] = chunks[q] + jnp.where(low_lanes, 0.0, piece)
            if q < 3:
                chunks[q + 1] = chunks[q + 1] + jnp.where(low_lanes, piece, 0.0)
        else:
            chunks[q] = chunks[q] + piece
    for q in range(4):
        cols = slice(128 * q, 128 * q + 128)
        total = None
        for k in range(FRACTIONS):
            line = chunks[q][k : k + 1, :]
            depv[k, :, cols] = line
            total = line if k == 0 else total + line
        bedo[:, cols] = bedv[:, cols] + total
    last = [
        pltpu.make_async_copy(depv, o_dep, out_sem.at[4]),
        pltpu.make_async_copy(bedo, o_bed, out_sem.at[5]),
    ]
    for copy in last:
        copy.start()

    for n, (sends, src, dst, device, _) in enumerate(plan):

        @pl.when(sends)
        def _(n=n, src=src, dst=dst, device=device):
            remote(src, dst, nb_send.at[n], nb_recv.at[n], device).wait_send()

    pltpu.make_async_copy(strips.at[pl.ds(0, 15)], band.at[pl.ds(0, 15)], st_send.at[0]).wait()

    @pl.when(jnp.logical_or(both(C <= 2, up), both(C >= COLS - 3, down)))
    def _():
        pltpu.make_async_copy(strips, band.at[pl.ds(0, 16)], st_send.at[1]).wait()

    @pl.when(left)
    def _():
        pltpu.make_async_copy(nsum, nrx.at[0], ns_send.at[0]).wait()

    @pl.when(right)
    def _():
        pltpu.make_async_copy(nsum, nrx.at[1], ns_send.at[1]).wait()

    pltpu.make_async_copy(tot.at[pl.ds(0, 120)], rs.at[pl.ds(0, 120)], ph_send).wait()
    for copy in stores + [fine_store] + last:
        copy.wait()


def local(water_depth, discharge, sediment, bed_level, cell_map, wet_mask, sediment_params):
    hbm = pl.BlockSpec(memory_space=pl.ANY)
    dma = pltpu.SemaphoreType.DMA
    bf16 = jnp.bfloat16
    scratch = [
        ((9, 80, 128), f32),
        ((2, 64, 128), i32),
        ((1, 512), f32),
        ((10, 8, 128), f32),
        ((2, 13, 8, 128), f32),
        ((16, 1, 128), f32),
        ((22, 1, 128), f32),
        ((24, 128), f32),
        ((80, 128), f32),
        ((2, 80, 128), f32),
        ((80, 128), i32),
        ((80, 128), i32),
        ((80, 128), i32),
        ((7, 14, 8, 256), f32),
        ((12, 8, 256), f32),
        ((10, 8, 256), f32),
        ((10, 8, 256), f32),
        ((11, 8, 256), f32),
        ((10, 8, 256), f32),
        ((10, 8, 256), f32),
        ((7, 8, 256), f32),
        ((7, 8, 256), f32),
        ((3, 4, 8, 128), f32),
        ((4, 10, 8, 128), f32),
        ((7, 80, 128), f32),
        ((4, 80, 128), f32),
        ((896, 128), bf16),
        ((192, 896), bf16),
        ((192, 896), bf16),
        ((128, 128), f32),
        ((16, 128), f32),
        ((2, 16, 128), f32),
        ((128, 128), f32),
        ((24, 128), f32),
        ((64, 128), f32),
        ((4, 1, 512), f32),
        ((1, 512), f32),
    ]
    return pl.pallas_call(
        kernel,
        out_shape=(
            jax.ShapeDtypeStruct((64, 128), f32),
            jax.ShapeDtypeStruct((2, 64, 128), f32),
            jax.ShapeDtypeStruct((4, 64, 128), f32),
            jax.ShapeDtypeStruct((64, 128), f32),
            jax.ShapeDtypeStruct((1, 512), f32),
            jax.ShapeDtypeStruct((4, 1, 512), f32),
        ),
        in_specs=[hbm] * 6 + [pl.BlockSpec(memory_space=pltpu.SMEM)],
        out_specs=(hbm,) * 6,
        scratch_shapes=[pltpu.VMEM(shape, dtype) for shape, dtype in scratch]
        + [dma((6,)), dma((8,)), dma((8,)), dma((2,)), dma((3,)), dma(()), dma(()), dma((2,)), dma((2,)), dma((6,))],
        compiler_params=pltpu.CompilerParams(
            collective_id=0, has_side_effects=True, vmem_limit_bytes=32 * 1024 * 1024
        ),
    )(water_depth, discharge, sediment, bed_level, cell_map, wet_mask, sediment_params)


def solution(mesh):
    placed = (
        P("row", "col"),
        P(None, "row", "col"),
        P(None, "row", "col"),
        P(("row", "col"), None),
        P("row", "col"),
        P("row", "col"),
        P(),
    )
    return jax.shard_map(
        local,
        mesh=mesh,
        in_specs=placed,
        out_specs=(
            P("row", "col"),
            P(None, "row", "col"),
            P(None, "row", "col"),
            P("row", "col"),
            P(("row", "col"), None),
            P(None, ("row", "col"), None),
        ),
        check_vma=False,
    )
```

time: 256 us -> 61.3 us (0.24)
  the two profiles are of different devices: /device:TPU:57 before, /device:TPU:1 now
where the time goes in v1:
time: 61.3 us; the launch traced here: 60.4 us
  Pallas kernels  50.7 us (83%)
  local copies, waits for them, and re-layouts  9.06 us (15%)
  between operations  0.66 us (1%)
    pallas_call x1, Pallas kernels, local(): pl.pallas_call(kernel, out_shape=(jax.ShapeDtypeStruct((64, 128), f32), j...  50.7 us
    unnamed x20, local copies, waits for them, and re-layouts  9.06 us

profile of v1, /device:TPU:1, one launch (start us, length us, event | category | flops | bytes accessed | tf_op | source)
XLA Modules:
  0.0 60.4 jit_solution(4973414130292304028)
XLA Ops:
  0.6 0.0 copy-start
  0.6 0.9 %copy-done = f32[4,64,128]{2,1,0:T(8,128)S(1)} copy-done((f32[4,64,128]{2,1,0:T(8,128)S(1)}, f32[4,64,128]{2,1,0:T(8,128)}, u32[]{:S(2)}) %copy-start) | copy-done | bytes 131096
  1.5 0.0 copy-start.1
  1.5 0.8 %copy-done.1 = f32[2,64,128]{2,1,0:T(8,128)S(1)} copy-done((f32[2,64,128]{2,1,0:T(8,128)S(1)}, f32[2,64,128]{2,1,0:T(8,128)}, u32[]{:S(2)}) %copy-start.1) | copy-done | bytes 65560
  2.4 0.0 copy-start.2
  2.4 0.8 %copy-done.2 = f32[64,128]{1,0:T(8,128)S(1)} copy-done((f32[64,128]{1,0:T(8,128)S(1)}, f32[64,128]{1,0:T(8,128)}, u32[]{:S(2)}) %copy-start.2) | copy-done | bytes 32792
  3.1 0.0 copy-start.3
  3.1 0.8 %copy-done.3 = s32[64,128]{1,0:T(8,128)S(1)} copy-done((s32[64,128]{1,0:T(8,128)S(1)}, s32[64,128]{1,0:T(8,128)}, u32[]{:S(2)}) %copy-start.3) | copy-done | bytes 32792
  3.9 0.0 copy-start.4
  3.9 0.8 %copy-done.4 = s32[64,128]{1,0:T(8,128)S(1)} copy-done((s32[64,128]{1,0:T(8,128)S(1)}, s32[64,128]{1,0:T(8,128)}, u32[]{:S(2)}) %copy-start.4) | copy-done | bytes 32792
  4.7 0.0 copy-start.5
  4.7 0.7 %copy-done.5 = f32[1,512]{1,0:T(1,128)S(1)} copy-done((f32[1,512]{1,0:T(1,128)S(1)}, f32[1,512]{1,0:T(1,128)}, u32[]{:S(2)}) %copy-start.5) | copy-done | bytes 2072
  5.3 0.0 copy-start.6
  5.3 0.7 %copy-done.6 = f32[3,4]{1,0:T(4,128)S(1)} copy-done((f32[3,4]{1,0:T(4,128)S(1)}, f32[3,4]{1,0:T(4,128)}, u32[]{:S(2)}) %copy-start.6) | copy-done | bytes 72
  6.0 50.7 %shard_map.118 = (f32[64,128]{1,0:T(8,128)S(1)}, f32[2,64,128]{2,1,0:T(8,128)S(1)}, f32[4,64,128]{2,1,0:T(8,128)S(1)}, f32[64,128]{1,0:T(8,128)S(1)}, f32[1,512]{1,0:T(1,128)S(1)}, /*index=5*/f32[4,1,512]{2,1,0:T(1,128)S(1)}) custom-call(f32[64,128]{1,0:T(8,128)S(1)} %copy-done.2, f32[2,64,128]{2,1,0:T(8,128)S(1)} %copy-done.1, f32[4,64,128]{2,1,0:T(8,128)S(1)} %copy-done, ...), custom_call_target="tpu_custom_call" | custom-call | tf_op jit(solution)/shard_map/pallas_call | solution.py:570
  56.8 0.6 %copy.19 = f32[64,128]{1,0:T(8,128)} copy(f32[64,128]{1,0:T(8,128)S(1)} %get-tuple-element.12) | data formatting | bytes 65536
  57.4 0.6 %copy.20 = f32[2,64,128]{2,1,0:T(8,128)} copy(f32[2,64,128]{2,1,0:T(8,128)S(1)} %get-tuple-element.13) | data formatting | bytes 131072
  58.0 0.7 %copy.21 = f32[4,64,128]{2,1,0:T(8,128)} copy(f32[4,64,128]{2,1,0:T(8,128)S(1)} %get-tuple-element.14) | data formatting | bytes 262144
  58.7 0.6 %copy.22 = f32[64,128]{1,0:T(8,128)} copy(f32[64,128]{1,0:T(8,128)S(1)} %get-tuple-element.15) | data formatting | bytes 65536
  59.3 0.6 copy.23
  59.8 0.6 copy.24
Async XLA Ops:
  0.6 0.9 %copy-start = (f32[4,64,128]{2,1,0:T(8,128)S(1)}, f32[4,64,128]{2,1,0:T(8,128)}, u32[]{:S(2)}) copy-start(f32[4,64,128]{2,1,0:T(8,128)} %sed.1) | copy-start | bytes 393220
  1.5 0.8 %copy-start.1 = (f32[2,64,128]{2,1,0:T(8,128)S(1)}, f32[2,64,128]{2,1,0:T(8,128)}, u32[]{:S(2)}) copy-start(f32[2,64,128]{2,1,0:T(8,128)} %disch.1) | copy-start | bytes 196612
  2.4 0.8 %copy-start.2 = (f32[64,128]{1,0:T(8,128)S(1)}, f32[64,128]{1,0:T(8,128)}, u32[]{:S(2)}) copy-start(f32[64,128]{1,0:T(8,128)} %depth.1) | copy-start | bytes 98308
  3.1 0.8 %copy-start.3 = (s32[64,128]{1,0:T(8,128)S(1)}, s32[64,128]{1,0:T(8,128)}, u32[]{:S(2)}) copy-start(s32[64,128]{1,0:T(8,128)} %cmap.1) | copy-start | bytes 98308
  3.9 0.8 %copy-start.4 = (s32[64,128]{1,0:T(8,128)S(1)}, s32[64,128]{1,0:T(8,128)}, u32[]{:S(2)}) copy-start(s32[64,128]{1,0:T(8,128)} %wetm.1) | copy-start | bytes 98308
  4.7 0.7 %copy-start.5 = (f32[1,512]{1,0:T(1,128)S(1)}, f32[1,512]{1,0:T(1,128)}, u32[]{:S(2)}) copy-start(f32[1,512]{1,0:T(1,128)} %bed.1) | copy-start | bytes 6148
  5.3 0.7 %copy-start.6 = (f32[3,4]{1,0:T(4,128)S(1)}, f32[3,4]{1,0:T(4,128)}, u32[]{:S(2)}) copy-start(f32[3,4]{1,0:T(4,128)} %par.1) | copy-start | bytes 148

commit v2 on v1

v2 whole, which is shorter than its diff:
```python
import jax
import jax.numpy as jnp
from jax import lax
from jax.experimental import pallas as pl
from jax.experimental.pallas import tpu as pltpu
from jax.sharding import PartitionSpec as P

FRACTIONS = 4
SUBSTEPS = 4
ROWS = 32
COLS = 16
MAIN, SIDE = 2, 16
SLOTS = 23

MESH = pl.DeviceIdType.MESH
f32 = jnp.float32
i32 = jnp.int32


def roll(x, shift, axis):
    return pltpu.roll(x, shift % x.shape[axis], axis)


def minmod(a, b):
    return jnp.maximum(jnp.minimum(b, 0.0), jnp.minimum(a, jnp.maximum(b, 0.0)))


def inverse(x):
    guess = pl.reciprocal(x, approx=True)
    return guess * (2.0 - x * guess)


def root(x):
    return x * lax.rsqrt(x + 1e-35)


def face_factors(h_l, n_l, h_r, n_r, opened):
    w_l = n_l * inverse(jnp.maximum(h_l, 2.5))
    w_r = n_r * inverse(jnp.maximum(h_r, 2.5))
    c_l = jnp.abs(w_l) + root(0.5 * h_l)
    c_r = jnp.abs(w_r) + root(0.5 * h_r)
    fastest = jnp.maximum(c_l, c_r)
    push = (0.25 * opened) * (h_l * h_l + h_r * h_r)
    return opened * (w_l + fastest), opened * (w_r - fastest), push


def kernel(
    depth, disch, sed, bed, cmap, wetm, par,
    o_depth, o_disch, o_sed, o_fine, o_bed, o_dep,
    nat, raw, bedv, pk, rx, strips, band, band2, cn, nbed,
    ibuf, rbuf, kbuf, fld, wet, bedp, gx, gy, ox, oy, wd, coef,
    exch, on, exn, sel, mhi, mlo, tot, nsum, nrx, rs, wnew, fineb, depv, bedo,
    in_sem, nb_send, nb_recv, st_send, st_recv, ph_send, ph_recv, ns_send, ns_recv, out_sem,
):
    R = lax.axis_index("row")
    C = lax.axis_index("col")
    other_half = jnp.where(C < 8, 8, 0)
    barrier = pltpu.get_barrier_semaphore()

    def greet(n, carry):
        c = (n + other_half) & 15
        near = jnp.abs(c - C) <= 1

        @pl.when(c != C)
        def _():
            pl.semaphore_signal(barrier, inc=1, device_id=(R, c), device_id_type=MESH)

        @pl.when(jnp.logical_and(R > 0, jnp.logical_or(near, c >= COLS - 3)))
        def _():
            pl.semaphore_signal(barrier, inc=1, device_id=(R - 1, c), device_id_type=MESH)

        @pl.when(jnp.logical_and(R < ROWS - 1, jnp.logical_or(near, c <= 2)))
        def _():
            pl.semaphore_signal(barrier, inc=1, device_id=(R + 1, c), device_id_type=MESH)

        return carry

    lax.fori_loop(0, COLS, greet, 0)

    mid = pl.ds(8, 64)
    loads = [
        pltpu.make_async_copy(depth, nat.at[0, mid], in_sem.at[0]),
        pltpu.make_async_copy(disch, nat.at[pl.ds(1, 2), mid], in_sem.at[1]),
        pltpu.make_async_copy(sed, nat.at[pl.ds(3, 4), mid], in_sem.at[2]),
        pltpu.make_async_copy(bed, bedv, in_sem.at[3]),
        pltpu.make_async_copy(cmap, raw.at[0], in_sem.at[4]),
        pltpu.make_async_copy(wetm, raw.at[1], in_sem.at[5]),
    ]
    for copy in loads:
        copy.start()

    lane = lax.broadcasted_iota(i32, (8, 128), 1)
    sub = lax.broadcasted_iota(i32, (8, 128), 0)
    low_lanes = lane < 64

    far = f32(1 << 20)

    @pl.when(R == 0)
    def _():
        nat[0:8, 0:8, :] = jnp.zeros((8, 8, 128), f32)
        nat[8, 0:8, :] = jnp.full((8, 128), far)
        band[0:3] = jnp.zeros((3, 1, 128), f32)

    @pl.when(R == ROWS - 1)
    def _():
        nat[0:8, 72:80, :] = jnp.zeros((8, 8, 128), f32)
        nat[8, 72:80, :] = jnp.full((8, 128), far)
        band[19:22] = jnp.zeros((3, 1, 128), f32)

    for side, edge in ((0, C == COLS - 1), (1, C == 0)):

        @pl.when(edge)
        def _(side=side):
            rx[side, 0] = jnp.full((8, 128), far)
            rx[side, 1:9] = jnp.zeros((8, 8, 128), f32)

        @pl.when(jnp.logical_or(edge, R == 0))
        def _(side=side):
            rx[side, 9] = jnp.zeros((8, 128), f32)
            rx[side, 10] = jnp.full((8, 128), far)

        @pl.when(jnp.logical_or(edge, R == ROWS - 1))
        def _(side=side):
            rx[side, 11] = jnp.full((8, 128), far)
            rx[side, 12] = jnp.zeros((8, 128), f32)

    @pl.when(C == COLS - 1)
    def _():
        nrx[0] = jnp.zeros((16, 128), f32)

    @pl.when(C == 0)
    def _():
        nrx[1] = jnp.zeros((16, 128), f32)

    wnew[...] = jnp.zeros((24, 128), f32)
    exch[...] = jnp.zeros(exch.shape, f32)

    from_col = lax.broadcasted_iota(i32, (128, 128), 0) // 4
    to_lane = lax.broadcasted_iota(i32, (128, 128), 1)
    for d in range(7):
        sel[128 * d : 128 * d + 128, :] = (
            jnp.where(to_lane - from_col == d + 5, 1.0, 0.0).astype(jnp.bfloat16)
        )

    for k in range(FRACTIONS):
        erode = 0.002 * jnp.full((8, 128), par[2, k], f32)
        coef[0, k] = 0.05 * jnp.full((8, 128), par[0, k], f32)
        coef[1, k] = erode / (0.05 * jnp.full((8, 128), par[1, k], f32))
        coef[2, k] = erode

    for copy in loads:
        copy.wait()
    nat[8, 8:72, :] = raw[0].astype(f32)
    nat[7, 8:72, :] = raw[1].astype(f32)

    at = 32 * lax.broadcasted_iota(i32, (16, 128), 0) - 8 + lax.broadcasted_iota(i32, (16, 128), 1)
    window = jnp.zeros((16, 128), f32)
    for q in range(4):
        chunk = jnp.broadcast_to(bedv[:, 128 * q : 128 * q + 128], (16, 128))
        got = jnp.take_along_axis(chunk, at & 127, axis=1, mode="promise_in_bounds")
        window = jnp.where((at >> 7) == q, got, window)
    for t in range(COLS):
        strips[t] = window[t : t + 1, :]

    map_pack = jnp.zeros((8, 128), f32)
    for g in range(8):
        rows = slice(8 + 8 * g, 16 + 8 * g)
        packed = jnp.zeros((8, 128), f32)
        for q in range(8):
            first = (lane >> 3) == 2 * q
            second = (lane >> 3) == 2 * q + 1
            values = nat[q, rows, :]
            packed = jnp.where(first, roll(values, 16 * q, 1), packed)
            packed = jnp.where(second, roll(values, 16 * q + 16, 1), packed)
        pk[1 + g] = packed
        values = nat[8, rows, :]
        map_pack = jnp.where((lane >> 3) == 2 * g, roll(values, 16 * g, 1), map_pack)
        map_pack = jnp.where((lane >> 3) == 2 * g + 1, roll(values, 16 * g + 16, 1), map_pack)
    pk[0] = map_pack
    pk[9] = map_pack

    up, down = R > 0, R < ROWS - 1
    left, right = C > 0, C < COLS - 1
    both = jnp.logical_and
    above = jnp.where(C <= 2, COLS, jnp.where(C == COLS - 1, 2, 3))
    below = jnp.where(C >= COLS - 3, COLS, jnp.where(C == 0, 2, 3))
    expected = COLS - 1 + jnp.where(up, above, 0) + jnp.where(down, below, 0)
    pl.semaphore_wait(barrier, expected)

    def remote(src, dst, send, recv, device):
        return pltpu.make_async_remote_copy(
            src_ref=src, dst_ref=dst, send_sem=send, recv_sem=recv,
            device_id=device, device_id_type=MESH,
        )

    plan = [
        (left, pk.at[pl.ds(0, 9)], rx.at[0, pl.ds(0, 9)], (R, C - 1), right),
        (right, pk.at[pl.ds(0, 9)], rx.at[1, pl.ds(0, 9)], (R, C + 1), left),
        (up, nat.at[:, pl.ds(8, 8)], nat.at[:, pl.ds(72, 8)], (R - 1, C), down),
        (down, nat.at[:, pl.ds(64, 8)], nat.at[:, pl.ds(0, 8)], (R + 1, C), up),
        (both(up, left), pk.at[pl.ds(0, 2)], rx.at[0, pl.ds(11, 2)], (R - 1, C - 1), both(down, right)),
        (both(up, right), pk.at[pl.ds(0, 2)], rx.at[1, pl.ds(11, 2)], (R - 1, C + 1), both(down, left)),
        (both(down, left), pk.at[pl.ds(8, 2)], rx.at[0, pl.ds(9, 2)], (R + 1, C - 1), both(up, right)),
        (both(down, right), pk.at[pl.ds(8, 2)], rx.at[1, pl.ds(9, 2)], (R + 1, C + 1), both(up, left)),
    ]

    def send_to_neighbours(which):
        for n in which:
            sends, src, dst, device, _ = plan[n]

            @pl.when(sends)
            def _(n=n, src=src, dst=dst, device=device):
                remote(src, dst, nb_send.at[n], nb_recv.at[n], device).start()

    def await_neighbours(which):
        for n in which:
            _, src, dst, device, gets = plan[n]

            @pl.when(gets)
            def _(n=n, src=src, dst=dst):
                pltpu.make_async_copy(src, dst, nb_recv.at[n]).wait()

    def send_strips(n, carry):
        t = (n + other_half) & 15

        @pl.when(t != C)
        def _():
            remote(strips.at[t], band.at[3 + C], st_send.at[0], st_recv.at[0], (R, t)).start()

        @pl.when(both(C <= 2, up))
        def _():
            remote(strips.at[t], band.at[19 + C], st_send.at[1], st_recv.at[1], (R - 1, t)).start()

        @pl.when(both(C >= COLS - 3, down))
        def _():
            remote(strips.at[t], band.at[C - 13], st_send.at[1], st_recv.at[2], (R + 1, t)).start()

        return carry

    send_to_neighbours((0, 1))
    lax.fori_loop(0, COLS // 2, send_strips, 0)
    send_to_neighbours(range(2, 8))
    lax.fori_loop(COLS // 2, COLS, send_strips, 0)
    band[3 + C] = strips[C]

    def main_plane(ref, t):
        return ref[pl.ds(t, 8, stride=10), :]

    def side_rows(ref, t):
        return ref[pl.ds(t, 8, stride=5), :], ref[pl.ds(40 + t, 8, stride=5), :]

    def side_inner(ref, t):
        a, b = side_rows(ref, t)
        low = jnp.where(lane < 32, roll(a, 8, 1), roll(a, -72, 1))
        high = jnp.where(lane < 96, roll(b, 72, 1), roll(b, -8, 1))
        return jnp.where(low_lanes, low, high)

    first_eight = (lane & 8) == 0
    seam = both(lane >= 56, lane < 72)
    halo_lanes = both(((lane + 8) & 63) < 16, lane >= 0)

    def side_halo(a, b, q, inner):
        one = roll(jnp.where(first_eight, a, b), 56 - 16 * q, 1)
        two = roll(jnp.where(first_eight, b, a), 120 - 16 * q, 1)
        return jnp.where(halo_lanes, jnp.where(seam, one, two), inner)

    def shifted(value, step, side):
        turned = roll(value, step, 0)
        if side:
            turned = jnp.where(sub == (0 if step == 1 else 7), roll(turned, 64, 1), turned)
        return turned

    def ghosts(ref, side):
        first, count = (SIDE, 5) if side else (MAIN, 10)
        ref[first - 2] = shifted(ref[first + count - 2], 1, side)
        ref[first - 1] = shifted(ref[first + count - 1], 1, side)
        ref[first + count] = shifted(ref[first], -1, side)
        ref[first + count + 1] = shifted(ref[first + 1], -1, side)

    def wet_factors(first, count):
        for s in range(first - 1, first + count):
            ox[s] = 0.05 * wet[s] * wet[s + 1]
        for s in range(first, first + count):
            oy[s] = 0.05 * wet[s] * roll(wet[s], -1, 1)
            wd[s] = 0.2 * wet[s]

    def chunk(src, dst, base, with_bed):
        kept = {}

        def q_at(q, s):
            if (q, s) not in kept:
                kept[q, s] = fld[src, q, base + s]
            return kept[q, s]

        diffs = {}

        def d_at(q, s):
            if (q, s) not in diffs:
                diffs[q, s] = q_at(q, s + 1) - q_at(q, s)
            return diffs[q, s]

        lefts, fluxes, twice = {}, {}, {}
        for s in range(-1, 6):
            rights = {}
            for q in range(7):
                slope = minmod(d_at(q, s - 1), d_at(q, s))
                double = q_at(q, s) + q_at(q, s)
                twice[q, s] = double
                lefts[q, s] = double + slope
                rights[q] = double - slope
            if s < 0:
                continue
            a, b, push = face_factors(
                lefts[0, s - 1], lefts[1, s - 1], rights[0], rights[1], ox[base + s - 1]
            )
            for q in range(7):
                flux = lefts[q, s - 1] * a + rights[q] * b
                fluxes[q, s] = flux + push if q == 1 else flux
            if s < 1:
                continue
            p = s - 1
            y_left, y_right = {}, {}
            for q in range(7):
                v = q_at(q, p)
                d = roll(v, -1, 1) - v
                slope = minmod(roll(d, 1, 1), d)
                y_left[q] = twice[q, p] + slope
                y_right[q] = roll(twice[q, p] - slope, -1, 1)
            a, b, push = face_factors(y_left[0], y_left[2], y_right[0], y_right[2], oy[base + p])
            new = []
            for q in range(7):
                flux = y_left[q] * a + y_right[q] * b
                if q == 2:
                    flux = flux + push
                net = (fluxes[q, s] - fluxes[q, p]) + (flux - roll(flux, 1, 1))
                new.append(q_at(q, p) - net)
            h = q_at(0, p)
            inv = inverse(jnp.maximum(h, 1.25))
            u, v = q_at(1, p) * inv, q_at(2, p) * inv
            s2 = u * u + v * v + 1e-6
            w = wd[base + p]
            drag = (0.02 * w) * root(s2)
            new[1] = new[1] - drag * u
            new[2] = new[2] - drag * v
            if with_bed:
                new[1] = new[1] + h * gx[base + p]
                new[2] = new[2] + h * gy[base + p]
            settle = inv * w
            for k in range(FRACTIONS):
                erosion = jnp.maximum(s2 * coef[1, k] - coef[2, k], 0.0)
                change = coef[0, k] * q_at(3 + k, p) * settle - erosion * w
                exch[k, base + p] += change
                new[3 + k] = new[3 + k] - change
            for q in range(7):
                fld[dst, q, base + p] = new[q]

    await_neighbours((2, 3))
    for t in range(10):
        for q in range(7):
            fld[0, q, MAIN + t] = main_plane(nat.at[q], t)
        wet[MAIN + t] = main_plane(nat.at[7], t)
    ghosts(wet, False)
    wet_factors(MAIN, 10)
    for q in range(7):
        ghosts(fld.at[0, q], False)
    for t in range(5):
        for q in range(7):
            fld[0, q, SIDE + t] = side_inner(nat.at[q], t)
        wet[SIDE + t] = side_inner(nat.at[7], t)

    def early(c, carry):
        chunk(0, 1, MAIN + 5 * c, False)
        return carry

    lax.fori_loop(0, 2, early, 0)

    await_neighbours((0, 1, 4, 5, 6, 7))
    for g in range(10):
        slot = 9 if g == 0 else (12 if g == 9 else g)
        cn[8 * g : 8 * g + 8, :] = jnp.where(first_eight, rx[0, slot], rx[1, slot])
    for t in range(5):
        a, b = side_rows(cn, t)
        for q in range(7):
            fld[0, q, SIDE + t] = side_halo(a, b, q, fld[0, q, SIDE + t])
        wet[SIDE + t] = side_halo(a, b, 7, wet[SIDE + t])
    ghosts(wet, True)
    wet_factors(SIDE, 5)
    for q in range(7):
        ghosts(fld.at[0, q], True)
    chunk(0, 1, SIDE, False)

    pltpu.make_async_copy(strips.at[pl.ds(0, 15)], band.at[pl.ds(3, 15)], st_recv.at[0]).wait()

    @pl.when(down)
    def _():
        pltpu.make_async_copy(strips.at[pl.ds(0, 3)], band.at[pl.ds(19, 3)], st_recv.at[1]).wait()

    @pl.when(up)
    def _():
        pltpu.make_async_copy(strips.at[pl.ds(0, 3)], band.at[pl.ds(0, 3)], st_recv.at[2]).wait()

    for e in range(22):
        band2[e : e + 1, :] = band[e]

    map_side = jnp.where(first_eight, rx[0, 0], rx[1, 0])
    map_top = jnp.where(first_eight, rx[0, 10], rx[1, 10])
    map_low = jnp.where(first_eight, rx[0, 11], rx[1, 11])
    top_half = sub < 4

    def looked_up(table, first_row, index, shift):
        rows = [jnp.broadcast_to(table[first_row + n : first_row + n + 1, :], (8, 128)) for n in range(4)]
        result = jnp.zeros((8, 128), f32)
        for n in range(3):
            pair = jnp.where(top_half, rows[n], rows[n + 1])
            got = jnp.take_along_axis(pair, index, axis=1, mode="promise_in_bounds")
            result = jnp.where(shift == n - 1, got, result)
        return result

    for g in range(10):
        rows = slice(8 * g, 8 * g + 8)
        if g == 0:
            beside = roll(map_top, -16 * 7, 1)
        elif g == 9:
            beside = map_low
        else:
            beside = roll(map_side, -16 * (g - 1), 1)
        for tile, values in enumerate((nat[8, rows, :], beside)):
            cells = values.astype(i32)
            base = 2 * g - 2 + (sub >> 2)
            shift = (cells >> 9) - base + (-16 if g == 0 else (16 if g == 9 else 0))
            index = ((cells & 511) - 32 * C + 8) & 127
            nbed[tile, rows, :] = looked_up(band2, 2 * g - 2 - 1 + 3, index, shift)
            if tile == 0:
                ibuf[rows, :] = index
                rbuf[rows, :] = shift
                kbuf[rows, :] = (shift + 1) * 7 + (index - 8 - (lane >> 2) + 3)

    for t in range(10):
        bedp[MAIN + t] = main_plane(nbed.at[0], t)
    for t in range(5):
        a, b = side_rows(nbed.at[1], t)
        bedp[SIDE + t] = side_halo(a, b, 0, side_inner(nbed.at[0], t))
    ghosts(bedp, False)
    ghosts(bedp, True)
    for first, count in ((MAIN, 10), (SIDE, 5)):
        for s in range(first, first + count):
            here = bedp[s]
            scale = -0.5 * wd[s]
            slope_x = scale * (bedp[s + 1] - bedp[s - 1])
            slope_y = scale * (roll(here, -1, 1) - roll(here, 1, 1))
            gx[s] = slope_x
            gy[s] = slope_y
            h = fld[0, 0, s]
            fld[1, 1, s] += h * slope_x
            fld[1, 2, s] += h * slope_y

    def substep(n, carry):
        src = n & 1
        for q in range(7):
            ghosts(fld.at[src, q], False)
            ghosts(fld.at[src, q], True)

        def part(c, inner):
            chunk(src, 1 - src, MAIN + 5 * c + 4 * (c // 2), True)
            return inner

        lax.fori_loop(0, 3, part, 0)
        return carry

    lax.fori_loop(1, SUBSTEPS, substep, 0)

    edge = jnp.logical_or(lane < 8, lane >= 120)

    def natural(planes, out):
        for t in range(10):
            out[pl.ds(t, 8, stride=10), :] = planes[MAIN + t]
        for t in range(5):
            value = planes[SIDE + t]
            for part, (to_left, to_right) in enumerate(((-8, 72), (-72, 8))):
                rows = pl.ds(40 * part + t, 8, stride=5)
                moved = jnp.where(low_lanes, roll(value, to_left, 1), roll(value, to_right, 1))
                out[rows, :] = jnp.where(edge, moved, out[rows, :])

    for k in range(FRACTIONS):
        natural(exch.at[k], exn.at[k])

    keys = [kbuf[pl.ds(8 + p, 16, stride=4), :] for p in range(4)]
    planes = [[exn[k, pl.ds(8 + p, 16, stride=4), :] for p in range(4)] for k in range(FRACTIONS)]
    for r in range(3):
        for d in range(7):
            hits = [keys[p] == r * 7 + d for p in range(4)]
            for k in range(FRACTIONS):
                acc = jnp.where(hits[0], planes[k][0], 0.0)
                for p in range(1, 4):
                    acc = acc + jnp.where(hits[p], planes[k][p], 0.0)
                high = acc.astype(jnp.bfloat16)
                rows = slice(64 * r + 16 * k, 64 * r + 16 * k + 16)
                mhi[rows, 128 * d : 128 * d + 128] = high
                mlo[rows, 128 * d : 128 * d + 128] = (acc - high.astype(f32)).astype(jnp.bfloat16)
    res = jnp.dot(mhi[...], sel[...], preferred_element_type=f32)
    res = res + jnp.dot(mlo[...], sel[...], preferred_element_type=f32)
    parts = []
    for k in range(FRACTIONS):
        part = res[64 + 16 * k : 80 + 16 * k]
        part = part + roll(res[16 * k : 16 * k + 16], -1, 0)
        part = part + roll(res[128 + 16 * k : 144 + 16 * k], 1, 0)
        parts.append(25.0 * part)
    nsum[...] = (parts[0] + parts[1]) + (parts[2] + parts[3])
    for n in range(2):
        pair = parts[2 * n] + roll(parts[2 * n + 1], 64, 1)
        for r in range(COLS):
            tot[r, :, 128 * n : 128 * n + 128] = pair[r : r + 1, :]

    def send_sums(n, carry):
        r = (n + other_half) & 15

        @pl.when(r != C)
        def _():
            remote(tot.at[r], rs.at[C], ph_send, ph_recv, (R, r)).start()

        return carry

    @pl.when(left)
    def _():
        remote(nsum, nrx.at[0], ns_send.at[0], ns_recv.at[0], (R, C - 1)).start()

    @pl.when(right)
    def _():
        remote(nsum, nrx.at[1], ns_send.at[1], ns_recv.at[1], (R, C + 1)).start()

    lax.fori_loop(0, COLS, send_sums, 0)
    rs[C] = tot[C]

    for q in range(7):
        natural(fld.at[0, q], on.at[q])
    stores = [
        pltpu.make_async_copy(on.at[0, mid], o_depth, out_sem.at[0]),
        pltpu.make_async_copy(on.at[pl.ds(1, 2), mid], o_disch, out_sem.at[1]),
        pltpu.make_async_copy(on.at[pl.ds(3, 4), mid], o_sed, out_sem.at[2]),
    ]
    for copy in stores:
        copy.start()

    for n, (sends, src, dst, device, _) in enumerate(plan):

        @pl.when(sends)
        def _(n=n, src=src, dst=dst, device=device):
            remote(src, dst, nb_send.at[n], nb_recv.at[n], device).wait_send()

    pltpu.make_async_copy(strips.at[pl.ds(0, 15)], band.at[pl.ds(0, 15)], st_send.at[0]).wait()

    @pl.when(jnp.logical_or(both(C <= 2, up), both(C >= COLS - 3, down)))
    def _():
        pltpu.make_async_copy(strips, band.at[pl.ds(0, 16)], st_send.at[1]).wait()

    @pl.when(right)
    def _():
        pltpu.make_async_copy(nsum, nrx.at[0], ns_recv.at[0]).wait()

    @pl.when(left)
    def _():
        pltpu.make_async_copy(nsum, nrx.at[1], ns_recv.at[1]).wait()

    wnew[1:17, :] = band2[3:19, :] + (nsum[...] + roll(nrx[0], 32, 1) + roll(nrx[1], -32, 1))
    for g in range(8):
        rows = slice(8 + 8 * g, 16 + 8 * g)
        fineb[8 * g : 8 * g + 8, :] = looked_up(wnew, 2 * g, ibuf[rows, :], rbuf[rows, :])
    fine_store = pltpu.make_async_copy(fineb, o_fine, out_sem.at[3])
    fine_store.start()

    pltpu.make_async_copy(tot.at[pl.ds(0, 15)], rs.at[pl.ds(0, 15)], ph_recv).wait()
    row_lane = lax.broadcasted_iota(i32, (1, 128), 1)
    row_low = row_lane < 64
    lines = [[jnp.zeros((1, 128), f32) for _ in range(4)] for _ in range(FRACTIONS)]
    for s in range(COLS):
        q, m = divmod(s, 4)
        for n in range(2):
            pair = rs[s, :, 128 * n : 128 * n + 128]
            for half in range(2):
                line = lines[2 * n + half]
                piece = jnp.where(row_low, 0.0, pair) if half else jnp.where(row_low, pair, 0.0)
                piece = roll(piece, 32 * m - 8 - 64 * half, 1)
                if m == 0:
                    line[q] = line[q] + jnp.where(row_low, piece, 0.0)
                    if q > 0:
                        line[q - 1] = line[q - 1] + jnp.where(row_low, 0.0, piece)
                elif m == 3:
                    line[q] = line[q] + jnp.where(row_low, 0.0, piece)
                    if q < 3:
                        line[q + 1] = line[q + 1] + jnp.where(row_low, piece, 0.0)
                else:
                    line[q] = line[q] + piece
    for q in range(4):
        cols = slice(128 * q, 128 * q + 128)
        total = None
        for k in range(FRACTIONS):
            line = lines[k][q]
            depv[k, :, cols] = line
            total = line if k == 0 else total + line
        bedo[:, cols] = bedv[:, cols] + total
    last = [
        pltpu.make_async_copy(depv, o_dep, out_sem.at[4]),
        pltpu.make_async_copy(bedo, o_bed, out_sem.at[5]),
    ]
    for copy in last:
        copy.start()

    @pl.when(left)
    def _():
        pltpu.make_async_copy(nsum, nrx.at[0], ns_send.at[0]).wait()

    @pl.when(right)
    def _():
        pltpu.make_async_copy(nsum, nrx.at[1], ns_send.at[1]).wait()

    pltpu.make_async_copy(tot.at[pl.ds(0, 15)], rs.at[pl.ds(0, 15)], ph_send).wait()
    for copy in stores + [fine_store] + last:
        copy.wait()


def handed_on(*refs):
    count = (len(refs) - 1) // 2
    copies = [pltpu.make_async_copy(refs[n], refs[count + n], refs[-1].at[n]) for n in range(count)]
    for copy in copies:
        copy.start()
    for copy in copies:
        copy.wait()


def local(water_depth, discharge, sediment, bed_level, cell_map, wet_mask, sediment_params):
    hbm = pl.BlockSpec(memory_space=pl.ANY)
    dma = pltpu.SemaphoreType.DMA
    bf16 = jnp.bfloat16
    plane = (SLOTS, 8, 128)
    scratch = [
        ((9, 80, 128), f32),
        ((2, 64, 128), i32),
        ((1, 512), f32),
        ((10, 8, 128), f32),
        ((2, 13, 8, 128), f32),
        ((16, 1, 128), f32),
        ((22, 1, 128), f32),
        ((24, 128), f32),
        ((80, 128), f32),
        ((2, 80, 128), f32),
        ((80, 128), i32),
        ((80, 128), i32),
        ((80, 128), i32),
        ((2, 7, *plane), f32),
        (plane, f32),
        (plane, f32),
        (plane, f32),
        (plane, f32),
        (plane, f32),
        (plane, f32),
        (plane, f32),
        ((3, 4, 8, 128), f32),
        ((4, *plane), f32),
        ((7, 80, 128), f32),
        ((4, 80, 128), f32),
        ((896, 128), bf16),
        ((192, 896), bf16),
        ((192, 896), bf16),
        ((16, 1, 256), f32),
        ((16, 128), f32),
        ((2, 16, 128), f32),
        ((16, 1, 256), f32),
        ((24, 128), f32),
        ((64, 128), f32),
        ((4, 1, 512), f32),
        ((1, 512), f32),
    ]
    results = tuple(
        jax.ShapeDtypeStruct(shape, f32)
        for shape in ((64, 128), (2, 64, 128), (4, 64, 128), (64, 128), (1, 512), (4, 1, 512))
    )
    made = pl.pallas_call(
        kernel,
        out_shape=results,
        in_specs=[hbm] * 6 + [pl.BlockSpec(memory_space=pltpu.SMEM)],
        out_specs=(hbm,) * 6,
        scratch_shapes=[pltpu.VMEM(shape, dtype) for shape, dtype in scratch]
        + [dma((6,)), dma((8,)), dma((8,)), dma((2,)), dma((3,)), dma(()), dma(()), dma((2,)), dma((2,)), dma((6,))],
        compiler_params=pltpu.CompilerParams(
            collective_id=0, has_side_effects=True, vmem_limit_bytes=56 * 1024 * 1024
        ),
    )(water_depth, discharge, sediment, bed_level, cell_map, wet_mask, sediment_params)
    return pl.pallas_call(
        handed_on,
        out_shape=results,
        in_specs=[hbm] * 6,
        out_specs=(hbm,) * 6,
        scratch_shapes=[dma((6,))],
        compiler_params=pltpu.CompilerParams(vmem_limit_bytes=56 * 1024 * 1024),
    )(*made)


def solution(mesh):
    placed = (
        P("row", "col"),
        P(None, "row", "col"),
        P(None, "row", "col"),
        P(("row", "col"), None),
        P("row", "col"),
        P("row", "col"),
        P(),
    )
    return jax.shard_map(
        local,
        mesh=mesh,
        in_specs=placed,
        out_specs=(
            P("row", "col"),
            P(None, "row", "col"),
            P(None, "row", "col"),
            P("row", "col"),
            P(("row", "col"), None),
            P(None, ("row", "col"), None),
        ),
        check_vma=False,
    )
```

time: 61.3 us -> 55.2 us (0.900); the launches traced: 60.4 us -> 55.1 us
  local copies, waits for them, and re-layouts: 9.06 us -> 0 us
  Pallas kernels: 50.7 us -> 54.4 us
    unnamed x20 -> x0, local copies, waits for them, and re-layouts: 9.06 us -> none
    pallas_call x1 -> x2, Pallas kernels: 50.7 us -> 54.4 us  [the longest x1 45 us: local(): pl.pallas_call(kernel, out_shape=results, in_specs=[hbm] * 6 + [pl.BlockS...]
where the time goes in v2:
time: 55.2 us; the launch traced here: 55.1 us
  Pallas kernels  54.4 us (99%)
  between operations  0.64 us (1%)
    pallas_call x1, Pallas kernels, local(): pl.pallas_call(kernel, out_shape=results, in_specs=[hbm] * 6 + [pl.BlockS...  45 us
    pallas_call x1, Pallas kernels, local(): pl.pallas_call(handed_on, out_shape=results, in_specs=[hbm] * 6, out_spec...  9.41 us

profile of v2, /device:TPU:1, one launch (start us, length us, event | category | flops | bytes accessed | tf_op | source)
XLA Modules:
  0.0 55.1 jit_solution(1295650963946029583)
XLA Ops:
  0.6 45.0 %shard_map.118 = (f32[64,128]{1,0:T(8,128)}, f32[2,64,128]{2,1,0:T(8,128)}, f32[4,64,128]{2,1,0:T(8,128)}, f32[64,128]{1,0:T(8,128)}, f32[1,512]{1,0:T(1,128)}, /*index=5*/f32[4,1,512]{2,1,0:T(1,128)}) custom-call(f32[64,128]{1,0:T(8,128)} %depth.1, f32[2,64,128]{2,1,0:T(8,128)} %disch.1, f32[4,64,128]{2,1,0:T(8,128)} %sed.1, f32[1,512]{1,0:T(1,128)} %bed.1, ...), custom_call_target="tpu_custom_call" | custom-call | tf_op jit(solution)/shard_map/pallas_call | solution.py:677
  45.6 9.4 %shard_map.119 = (f32[64,128]{1,0:T(8,128)}, f32[2,64,128]{2,1,0:T(8,128)}, f32[4,64,128]{2,1,0:T(8,128)}, f32[64,128]{1,0:T(8,128)}, f32[1,512]{1,0:T(1,128)}, /*index=5*/f32[4,1,512]{2,1,0:T(1,128)}) custom-call(f32[64,128]{1,0:T(8,128)} %get-tuple-element.12.refs_0_, f32[2,64,128]{2,1,0:T(8,128)} %get-tuple-element.13.refs_1_, ...), custom_call_target="tpu_custom_call" | custom-call | tf_op jit(solution)/shard_map/pallas_call | solution.py:688

commit v3 on v2

--- a/solution.py
+++ b/solution.py
@@ -46,11 +46,11 @@
 
 def kernel(
     depth, disch, sed, bed, cmap, wetm, par,
-    o_depth, o_disch, o_sed, o_fine, o_bed, o_dep,
-    nat, raw, bedv, pk, rx, strips, band, band2, cn, nbed,
-    ibuf, rbuf, kbuf, fld, wet, bedp, gx, gy, ox, oy, wd, coef,
-    exch, on, exn, sel, mhi, mlo, tot, nsum, nrx, rs, wnew, fineb, depv, bedo,
-    in_sem, nb_send, nb_recv, st_send, st_recv, ph_send, ph_recv, ns_send, ns_recv, out_sem,
+    o_fields, o_fine, o_bed, o_dep,
+    nat, raw, bedv, pk, rx, strips, band, band2, cn, nbed, sidx, sshift,
+    ibuf, rbuf, kbuf, one, two, wet, gx, gy, ox, oy, wd, coef,
+    exch, nmain, nside, sel, mhi, mlo, tot, nsum, nrx, rs, wnew,
+    in_sem, nb_send, nb_recv, st_send, st_recv, ph_send, ph_recv, ns_send, ns_recv,
 ):
     R = lax.axis_index("row")
     C = lax.axis_index("col")
@@ -133,7 +133,6 @@
         nrx[1] = jnp.zeros((16, 128), f32)
 
     wnew[...] = jnp.zeros((24, 128), f32)
-    exch[...] = jnp.zeros(exch.shape, f32)
 
     from_col = lax.broadcasted_iota(i32, (128, 128), 0) // 4
     to_lane = lax.broadcasted_iota(i32, (128, 128), 1)
@@ -249,20 +248,27 @@
     def side_rows(ref, t):
         return ref[pl.ds(t, 8, stride=5), :], ref[pl.ds(40 + t, 8, stride=5), :]
 
-    def side_inner(ref, t):
-        a, b = side_rows(ref, t)
-        low = jnp.where(lane < 32, roll(a, 8, 1), roll(a, -72, 1))
-        high = jnp.where(lane < 96, roll(b, 72, 1), roll(b, -8, 1))
-        return jnp.where(low_lanes, low, high)
+    def side_inner(ref):
+        rows = [side_rows(ref, t) for t in range(5)]
+        turned = [(roll(a, 8, 1), roll(a, -72, 1), roll(b, 72, 1), roll(b, -8, 1)) for a, b in rows]
+        return [
+            jnp.where(low_lanes, jnp.where(lane < 32, a, b), jnp.where(lane < 96, c, d))
+            for a, b, c, d in turned
+        ]
 
     first_eight = (lane & 8) == 0
     seam = both(lane >= 56, lane < 72)
     halo_lanes = both(((lane + 8) & 63) < 16, lane >= 0)
 
-    def side_halo(a, b, q, inner):
-        one = roll(jnp.where(first_eight, a, b), 56 - 16 * q, 1)
-        two = roll(jnp.where(first_eight, b, a), 120 - 16 * q, 1)
-        return jnp.where(halo_lanes, jnp.where(seam, one, two), inner)
+    def side_halo(mixed, q, inner):
+        turned = [(roll(a, 56 - 16 * q, 1), roll(b, 120 - 16 * q, 1)) for a, b in mixed]
+        return [
+            jnp.where(halo_lanes, jnp.where(seam, a, b), old) for (a, b), old in zip(turned, inner)
+        ]
+
+    def mixed_rows(ref):
+        rows = [side_rows(ref, t) for t in range(5)]
+        return [(jnp.where(first_eight, a, b), jnp.where(first_eight, b, a)) for a, b in rows]
 
     def shifted(value, step, side):
         turned = roll(value, step, 0)
@@ -270,37 +276,74 @@
             turned = jnp.where(sub == (0 if step == 1 else 7), roll(turned, 64, 1), turned)
         return turned
 
-    def ghosts(ref, side):
+    def around(planes, side):
+        return [
+            shifted(planes[-2], 1, side), shifted(planes[-1], 1, side),
+            shifted(planes[0], -1, side), shifted(planes[1], -1, side),
+        ]
+
+    def ghosts(ref, side, channels=range(7)):
         first, count = (SIDE, 5) if side else (MAIN, 10)
-        ref[first - 2] = shifted(ref[first + count - 2], 1, side)
-        ref[first - 1] = shifted(ref[first + count - 1], 1, side)
-        ref[first + count] = shifted(ref[first], -1, side)
-        ref[first + count + 1] = shifted(ref[first + 1], -1, side)
-
-    def wet_factors(first, count):
-        for s in range(first - 1, first + count):
-            ox[s] = 0.05 * wet[s] * wet[s + 1]
-        for s in range(first, first + count):
-            oy[s] = 0.05 * wet[s] * roll(wet[s], -1, 1)
-            wd[s] = 0.2 * wet[s]
-
-    def chunk(src, dst, base, with_bed):
-        kept = {}
+        made = [
+            around([ref[q, first + n] for n in (0, 1, count - 2, count - 1)], side) for q in channels
+        ]
+        for q, values in zip(channels, made):
+            for slot, value in zip((first - 2, first - 1, first + count, first + count + 1), values):
+                ref[q, slot] = value
+
+    def wet_factors(planes, side):
+        first, count = (SIDE, 5) if side else (MAIN, 10)
+        beyond = around(planes, side)
+        padded = [beyond[1]] + planes + [beyond[2]]
+        turned = [roll(w, -1, 1) for w in planes]
+        for n in range(count + 1):
+            ox[first - 1 + n] = 0.05 * padded[n] * padded[n + 1]
+        for n in range(count):
+            oy[first + n] = 0.05 * planes[n] * turned[n]
+            wd[first + n] = 0.2 * planes[n]
+
+    def chunk(src, dst, base, with_bed, start=False):
+        kept, diffs = {}, {}
 
         def q_at(q, s):
             if (q, s) not in kept:
-                kept[q, s] = fld[src, q, base + s]
+                kept[q, s] = src[q, base + s]
             return kept[q, s]
-
-        diffs = {}
 
         def d_at(q, s):
             if (q, s) not in diffs:
                 diffs[q, s] = q_at(q, s + 1) - q_at(q, s)
             return diffs[q, s]
 
+        ahead = {}
+
+        def fetch(p):
+            for q in range(7):
+                q_at(q, p + 2)
+            ahead[p] = [
+                tuple(roll(q_at(q, p), step, 1) for step in (1, -1, -2)) for q in range(7)
+            ]
+            if not start:
+                ahead[p, "sum"] = [exch[k, base + p] for k in range(FRACTIONS)]
+
+        def finish(p, new, turned, changes):
+            for q in range(7):
+                dst[q, base + p] = new[q] + turned[q]
+            for k in range(FRACTIONS):
+                exch[k, base + p] = changes[k]
+
+        for s in range(-2, 2):
+            for q in range(7):
+                q_at(q, s)
+        fetch(0)
         lefts, fluxes, twice = {}, {}, {}
+        pending = None
         for s in range(-1, 6):
+            if 1 <= s < 5:
+                fetch(s)
+            elif s == 5:
+                for q in range(7):
+                    q_at(q, 6)
             rights = {}
             for q in range(7):
                 slope = minmod(d_at(q, s - 1), d_at(q, s))
@@ -322,18 +365,18 @@
             y_left, y_right = {}, {}
             for q in range(7):
                 v = q_at(q, p)
-                d = roll(v, -1, 1) - v
-                slope = minmod(roll(d, 1, 1), d)
-                y_left[q] = twice[q, p] + slope
-                y_right[q] = roll(twice[q, p] - slope, -1, 1)
+                lower, upper, second = ahead[p][q]
+                d = upper - v
+                y_left[q] = twice[q, p] + minmod(v - lower, d)
+                y_right[q] = upper + upper - minmod(d, second - upper)
             a, b, push = face_factors(y_left[0], y_left[2], y_right[0], y_right[2], oy[base + p])
-            new = []
+            new, turned = [], []
             for q in range(7):
                 flux = y_left[q] * a + y_right[q] * b
                 if q == 2:
                     flux = flux + push
-                net = (fluxes[q, s] - fluxes[q, p]) + (flux - roll(flux, 1, 1))
-                new.append(q_at(q, p) - net)
+                turned.append(roll(flux, 1, 1))
+                new.append(q_at(q, p) - ((fluxes[q, s] - fluxes[q, p]) + flux))
             h = q_at(0, p)
             inv = inverse(jnp.maximum(h, 1.25))
             u, v = q_at(1, p) * inv, q_at(2, p) * inv
@@ -346,146 +389,179 @@
                 new[1] = new[1] + h * gx[base + p]
                 new[2] = new[2] + h * gy[base + p]
             settle = inv * w
+            changes = []
             for k in range(FRACTIONS):
                 erosion = jnp.maximum(s2 * coef[1, k] - coef[2, k], 0.0)
                 change = coef[0, k] * q_at(3 + k, p) * settle - erosion * w
-                exch[k, base + p] += change
                 new[3 + k] = new[3 + k] - change
-            for q in range(7):
-                fld[dst, q, base + p] = new[q]
+                changes.append(change if start else ahead[p, "sum"][k] + change)
+            if pending is not None:
+                finish(*pending)
+            pending = (p, new, turned, changes)
+        finish(*pending)
 
     await_neighbours((2, 3))
-    for t in range(10):
-        for q in range(7):
-            fld[0, q, MAIN + t] = main_plane(nat.at[q], t)
-        wet[MAIN + t] = main_plane(nat.at[7], t)
-    ghosts(wet, False)
-    wet_factors(MAIN, 10)
+    wet_main = [main_plane(nat.at[7], t) for t in range(10)]
+    wet_factors(wet_main, False)
     for q in range(7):
-        ghosts(fld.at[0, q], False)
-    for t in range(5):
-        for q in range(7):
-            fld[0, q, SIDE + t] = side_inner(nat.at[q], t)
-        wet[SIDE + t] = side_inner(nat.at[7], t)
+        planes = [main_plane(nat.at[q], t) for t in range(10)]
+        for t in range(10):
+            one[q, MAIN + t] = planes[t]
+    ghosts(one, False)
+    for q in range(8):
+        planes = side_inner(nat.at[q])
+        for t in range(5):
+            if q < 7:
+                one[q, SIDE + t] = planes[t]
+            else:
+                wet[SIDE + t] = planes[t]
+
+    top_half = sub < 4
+
+    def place(values, g):
+        cells = values.astype(i32)
+        base = 2 * g - 2 + (sub >> 2)
+        shift = (cells >> 9) - base + (-16 if g == 0 else (16 if g == 9 else 0))
+        return ((cells & 511) - 32 * C + 8) & 127, shift
+
+    places = [place(nat[8, 8 * g : 8 * g + 8, :], g) for g in range(10)]
+    for g, (index, shift) in enumerate(places):
+        rows = slice(8 * g, 8 * g + 8)
+        ibuf[rows, :] = index
+        rbuf[rows, :] = shift
+        kbuf[rows, :] = (shift + 1) * 7 + (index - 8 - (lane >> 2) + 3)
 
     def early(c, carry):
-        chunk(0, 1, MAIN + 5 * c, False)
+        chunk(one, two, MAIN + 5 * c, False, True)
         return carry
 
     lax.fori_loop(0, 2, early, 0)
 
     await_neighbours((0, 1, 4, 5, 6, 7))
-    for g in range(10):
-        slot = 9 if g == 0 else (12 if g == 9 else g)
-        cn[8 * g : 8 * g + 8, :] = jnp.where(first_eight, rx[0, slot], rx[1, slot])
-    for t in range(5):
-        a, b = side_rows(cn, t)
-        for q in range(7):
-            fld[0, q, SIDE + t] = side_halo(a, b, q, fld[0, q, SIDE + t])
-        wet[SIDE + t] = side_halo(a, b, 7, wet[SIDE + t])
-    ghosts(wet, True)
-    wet_factors(SIDE, 5)
-    for q in range(7):
-        ghosts(fld.at[0, q], True)
-    chunk(0, 1, SIDE, False)
-
-    pltpu.make_async_copy(strips.at[pl.ds(0, 15)], band.at[pl.ds(3, 15)], st_recv.at[0]).wait()
-
-    @pl.when(down)
-    def _():
-        pltpu.make_async_copy(strips.at[pl.ds(0, 3)], band.at[pl.ds(19, 3)], st_recv.at[1]).wait()
-
-    @pl.when(up)
-    def _():
-        pltpu.make_async_copy(strips.at[pl.ds(0, 3)], band.at[pl.ds(0, 3)], st_recv.at[2]).wait()
-
-    for e in range(22):
-        band2[e : e + 1, :] = band[e]
-
+    slots = [9, *range(1, 9), 12]
+    side_values = [jnp.where(first_eight, rx[0, slot], rx[1, slot]) for slot in slots]
     map_side = jnp.where(first_eight, rx[0, 0], rx[1, 0])
     map_top = jnp.where(first_eight, rx[0, 10], rx[1, 10])
     map_low = jnp.where(first_eight, rx[0, 11], rx[1, 11])
-    top_half = sub < 4
-
-    def looked_up(table, first_row, index, shift):
-        rows = [jnp.broadcast_to(table[first_row + n : first_row + n + 1, :], (8, 128)) for n in range(4)]
-        result = jnp.zeros((8, 128), f32)
-        for n in range(3):
-            pair = jnp.where(top_half, rows[n], rows[n + 1])
-            got = jnp.take_along_axis(pair, index, axis=1, mode="promise_in_bounds")
-            result = jnp.where(shift == n - 1, got, result)
-        return result
-
+    beside = [map_top] + [map_side] * 8 + [map_low]
+    beside = [roll(v, -16 * n, 1) for v, n in zip(beside, (7, *range(8), 0))]
+    places = [place(values, g) for g, values in enumerate(beside)]
     for g in range(10):
-        rows = slice(8 * g, 8 * g + 8)
-        if g == 0:
-            beside = roll(map_top, -16 * 7, 1)
-        elif g == 9:
-            beside = map_low
-        else:
-            beside = roll(map_side, -16 * (g - 1), 1)
-        for tile, values in enumerate((nat[8, rows, :], beside)):
-            cells = values.astype(i32)
-            base = 2 * g - 2 + (sub >> 2)
-            shift = (cells >> 9) - base + (-16 if g == 0 else (16 if g == 9 else 0))
-            index = ((cells & 511) - 32 * C + 8) & 127
-            nbed[tile, rows, :] = looked_up(band2, 2 * g - 2 - 1 + 3, index, shift)
-            if tile == 0:
-                ibuf[rows, :] = index
-                rbuf[rows, :] = shift
-                kbuf[rows, :] = (shift + 1) * 7 + (index - 8 - (lane >> 2) + 3)
-
-    for t in range(10):
-        bedp[MAIN + t] = main_plane(nbed.at[0], t)
-    for t in range(5):
-        a, b = side_rows(nbed.at[1], t)
-        bedp[SIDE + t] = side_halo(a, b, 0, side_inner(nbed.at[0], t))
-    ghosts(bedp, False)
-    ghosts(bedp, True)
-    for first, count in ((MAIN, 10), (SIDE, 5)):
-        for s in range(first, first + count):
-            here = bedp[s]
-            scale = -0.5 * wd[s]
-            slope_x = scale * (bedp[s + 1] - bedp[s - 1])
-            slope_y = scale * (roll(here, -1, 1) - roll(here, 1, 1))
-            gx[s] = slope_x
-            gy[s] = slope_y
-            h = fld[0, 0, s]
-            fld[1, 1, s] += h * slope_x
-            fld[1, 2, s] += h * slope_y
-
-    def substep(n, carry):
-        src = n & 1
-        for q in range(7):
-            ghosts(fld.at[src, q], False)
-            ghosts(fld.at[src, q], True)
-
-        def part(c, inner):
-            chunk(src, 1 - src, MAIN + 5 * c + 4 * (c // 2), True)
-            return inner
-
-        lax.fori_loop(0, 3, part, 0)
-        return carry
-
-    lax.fori_loop(1, SUBSTEPS, substep, 0)
+        cn[8 * g : 8 * g + 8, :] = side_values[g]
+        sidx[8 * g : 8 * g + 8, :], sshift[8 * g : 8 * g + 8, :] = places[g]
+    mixed = mixed_rows(cn)
+    wet_side = side_halo(mixed, 7, [wet[SIDE + t] for t in range(5)])
+    whole = [side_halo(mixed, q, [one[q, SIDE + t] for t in range(5)]) for q in range(7)]
+    wet_factors(wet_side, True)
+    for q in range(7):
+        for t in range(5):
+            one[q, SIDE + t] = whole[q][t]
+    ghosts(one, True)
+    chunk(one, two, SIDE, False, True)
+    ghosts(two, False, (0, 3, 4, 5, 6))
+    ghosts(two, True, (0, 3, 4, 5, 6))
+
+    pltpu.make_async_copy(strips.at[pl.ds(0, 15)], band.at[pl.ds(3, 15)], st_recv.at[0]).wait()
+
+    @pl.when(down)
+    def _():
+        pltpu.make_async_copy(strips.at[pl.ds(0, 3)], band.at[pl.ds(19, 3)], st_recv.at[1]).wait()
+
+    @pl.when(up)
+    def _():
+        pltpu.make_async_copy(strips.at[pl.ds(0, 3)], band.at[pl.ds(0, 3)], st_recv.at[2]).wait()
+
+    band_rows = [band[e] for e in range(22)]
+    for e in range(22):
+        band2[e : e + 1, :] = band_rows[e]
+
+    def wide_rows(table, first_row, count):
+        return [
+            jnp.broadcast_to(table[first_row + n : first_row + n + 1, :], (8, 128)) for n in range(count)
+        ]
+
+    def looked_up(rows, places):
+        found = []
+        for g, (index, shift) in enumerate(places):
+            found.append([
+                jnp.take_along_axis(
+                    jnp.where(top_half, rows[2 * g + n], rows[2 * g + n + 1]),
+                    index, axis=1, mode="promise_in_bounds",
+                )
+                for n in range(3)
+            ])
+        return [
+            jnp.where(
+                shift == -1, got[0],
+                jnp.where(shift == 0, got[1], jnp.where(shift == 1, got[2], 0.0)),
+            )
+            for got, (_, shift) in zip(found, places)
+        ]
+
+    rows = wide_rows(band2, 0, 22)
+    groups = [slice(8 * g, 8 * g + 8) for g in range(10)]
+    found = looked_up(rows, [(ibuf[r, :], rbuf[r, :]) for r in groups])
+    for r, value in zip(groups, found):
+        nbed[0, r, :] = value
+    found = looked_up(rows, [(sidx[r, :], sshift[r, :]) for r in groups])
+    for r, value in zip(groups, found):
+        nbed[1, r, :] = value
+
+    bed_main = [main_plane(nbed.at[0], t) for t in range(10)]
+    bed_side = side_halo(mixed_rows(nbed.at[1]), 0, side_inner(nbed.at[0]))
+    for planes, side in ((bed_main, False), (bed_side, True)):
+        first, count = (SIDE, 5) if side else (MAIN, 10)
+        beyond = around(planes, side)
+        padded = [beyond[1]] + planes + [beyond[2]]
+        turned = [(roll(v, -1, 1), roll(v, 1, 1)) for v in planes]
+        scale = [-0.5 * wd[first + n] for n in range(count)]
+        slope_x = [scale[n] * (padded[n + 2] - padded[n]) for n in range(count)]
+        slope_y = [scale[n] * (turned[n][0] - turned[n][1]) for n in range(count)]
+        depths = [one[0, first + n] for n in range(count)]
+        new_x = [two[1, first + n] + depths[n] * slope_x[n] for n in range(count)]
+        new_y = [two[2, first + n] + depths[n] * slope_y[n] for n in range(count)]
+        for n in range(count):
+            gx[first + n] = slope_x[n]
+            gy[first + n] = slope_y[n]
+            two[1, first + n] = new_x[n]
+            two[2, first + n] = new_y[n]
+    ghosts(two, False, (1, 2))
+    ghosts(two, True, (1, 2))
+
+    for substep in range(1, SUBSTEPS):
+        src, dst = (two, one) if substep % 2 else (one, two)
+
+        def each(c, carry, src=src, dst=dst):
+            chunk(src, dst, MAIN + 5 * c + 4 * (c // 2), True)
+            return carry
+
+        lax.fori_loop(0, 3, each, 0)
+        if substep < SUBSTEPS - 1:
+            ghosts(dst, False)
+            ghosts(dst, True)
 
     edge = jnp.logical_or(lane < 8, lane >= 120)
 
-    def natural(planes, out):
-        for t in range(10):
-            out[pl.ds(t, 8, stride=10), :] = planes[MAIN + t]
-        for t in range(5):
-            value = planes[SIDE + t]
-            for part, (to_left, to_right) in enumerate(((-8, 72), (-72, 8))):
-                rows = pl.ds(40 * part + t, 8, stride=5)
-                moved = jnp.where(low_lanes, roll(value, to_left, 1), roll(value, to_right, 1))
-                out[rows, :] = jnp.where(edge, moved, out[rows, :])
+    def natural(planes, n):
+        mains = [planes[MAIN + t] for t in range(10)]
+        sides = [planes[SIDE + t] for t in range(5)]
+        turned = [tuple(roll(v, step, 1) for step in (-8, 72, -72, 8)) for v in sides]
+        for t, value in enumerate(mains):
+            nmain[n, pl.ds(t, 8, stride=10), :] = value
+        for t, (a, b, c, d) in enumerate(turned):
+            nside[n, pl.ds(t, 8, stride=5), :] = jnp.where(low_lanes, a, b)
+            nside[n, pl.ds(40 + t, 8, stride=5), :] = jnp.where(low_lanes, c, d)
 
     for k in range(FRACTIONS):
-        natural(exch.at[k], exn.at[k])
+        natural(exch.at[k], k)
+    wide_edge = jnp.concatenate([edge, edge], axis=0)
 
     keys = [kbuf[pl.ds(8 + p, 16, stride=4), :] for p in range(4)]
-    planes = [[exn[k, pl.ds(8 + p, 16, stride=4), :] for p in range(4)] for k in range(FRACTIONS)]
+    fourth = [pl.ds(8 + p, 16, stride=4) for p in range(4)]
+    planes = [
+        [jnp.where(wide_edge, nside[k, rows, :], nmain[k, rows, :]) for rows in fourth]
+        for k in range(FRACTIONS)
+    ]
     for r in range(3):
         for d in range(7):
             hits = [keys[p] == r * 7 + d for p in range(4)]
@@ -532,14 +608,11 @@
     rs[C] = tot[C]
 
     for q in range(7):
-        natural(fld.at[0, q], on.at[q])
-    stores = [
-        pltpu.make_async_copy(on.at[0, mid], o_depth, out_sem.at[0]),
-        pltpu.make_async_copy(on.at[pl.ds(1, 2), mid], o_disch, out_sem.at[1]),
-        pltpu.make_async_copy(on.at[pl.ds(3, 4), mid], o_sed, out_sem.at[2]),
-    ]
-    for copy in stores:
-        copy.start()
+        natural(one.at[q], 4 + q)
+    for q in range(7):
+        for g in range(1, 9):
+            rows = slice(8 * g, 8 * g + 8)
+            o_fields[q, rows, :] = jnp.where(edge, nside[4 + q, rows, :], nmain[4 + q, rows, :])
 
     for n, (sends, src, dst, device, _) in enumerate(plan):
 
@@ -562,11 +635,10 @@
         pltpu.make_async_copy(nsum, nrx.at[1], ns_recv.at[1]).wait()
 
     wnew[1:17, :] = band2[3:19, :] + (nsum[...] + roll(nrx[0], 32, 1) + roll(nrx[1], -32, 1))
-    for g in range(8):
-        rows = slice(8 + 8 * g, 16 + 8 * g)
-        fineb[8 * g : 8 * g + 8, :] = looked_up(wnew, 2 * g, ibuf[rows, :], rbuf[rows, :])
-    fine_store = pltpu.make_async_copy(fineb, o_fine, out_sem.at[3])
-    fine_store.start()
+    inner = [slice(8 + 8 * g, 16 + 8 * g) for g in range(8)]
+    found = looked_up(wide_rows(wnew, 0, 18), [(ibuf[r, :], rbuf[r, :]) for r in inner])
+    for g, value in enumerate(found):
+        o_fine[8 * g : 8 * g + 8, :] = value
 
     pltpu.make_async_copy(tot.at[pl.ds(0, 15)], rs.at[pl.ds(0, 15)], ph_recv).wait()
     row_lane = lax.broadcasted_iota(i32, (1, 128), 1)
@@ -595,16 +667,9 @@
         total = None
         for k in range(FRACTIONS):
             line = lines[k][q]
-            depv[k, :, cols] = line
+            o_dep[k, :, cols] = line
             total = line if k == 0 else total + line
-        bedo[:, cols] = bedv[:, cols] + total
-    last = [
-        pltpu.make_async_copy(depv, o_dep, out_sem.at[4]),
-        pltpu.make_async_copy(bedo, o_bed, out_sem.at[5]),
-    ]
-    for copy in last:
-        copy.start()
-
+        o_bed[:, cols] = bedv[:, cols] + total
     @pl.when(left)
     def _():
         pltpu.make_async_copy(nsum, nrx.at[0], ns_send.at[0]).wait()
@@ -614,13 +679,19 @@
         pltpu.make_async_copy(nsum, nrx.at[1], ns_send.at[1]).wait()
 
     pltpu.make_async_copy(tot.at[pl.ds(0, 15)], rs.at[pl.ds(0, 15)], ph_send).wait()
-    for copy in stores + [fine_store] + last:
-        copy.wait()
-
-
-def handed_on(*refs):
-    count = (len(refs) - 1) // 2
-    copies = [pltpu.make_async_copy(refs[n], refs[count + n], refs[-1].at[n]) for n in range(count)]
+
+
+def handed_on(fields, fine, bed, dep, o_depth, o_disch, o_sed, o_fine, o_bed, o_dep, sem):
+    mid = pl.ds(8, 64)
+    pairs = (
+        (fields.at[0, mid], o_depth),
+        (fields.at[pl.ds(1, 2), mid], o_disch),
+        (fields.at[pl.ds(3, 4), mid], o_sed),
+        (fine, o_fine),
+        (bed, o_bed),
+        (dep, o_dep),
+    )
+    copies = [pltpu.make_async_copy(src, dst, sem.at[n]) for n, (src, dst) in enumerate(pairs)]
     for copy in copies:
         copy.start()
     for copy in copies:
@@ -630,6 +701,7 @@
 def local(water_depth, discharge, sediment, bed_level, cell_map, wet_mask, sediment_params):
     hbm = pl.BlockSpec(memory_space=pl.ANY)
     dma = pltpu.SemaphoreType.DMA
+    vmem = pl.BlockSpec(memory_space=pltpu.VMEM)
     bf16 = jnp.bfloat16
     plane = (SLOTS, 8, 128)
     scratch = [
@@ -646,8 +718,10 @@
         ((80, 128), i32),
         ((80, 128), i32),
         ((80, 128), i32),
-        ((2, 7, *plane), f32),
-        (plane, f32),
+        ((80, 128), i32),
+        ((80, 128), i32),
+        ((7, *plane), f32),
+        ((7, *plane), f32),
         (plane, f32),
         (plane, f32),
         (plane, f32),
@@ -656,8 +730,8 @@
         (plane, f32),
         ((3, 4, 8, 128), f32),
         ((4, *plane), f32),
-        ((7, 80, 128), f32),
-        ((4, 80, 128), f32),
+        ((11, 80, 128), f32),
+        ((11, 80, 128), f32),
         ((896, 128), bf16),
         ((192, 896), bf16),
         ((192, 896), bf16),
@@ -666,9 +740,6 @@
         ((2, 16, 128), f32),
         ((16, 1, 256), f32),
         ((24, 128), f32),
-        ((64, 128), f32),
-        ((4, 1, 512), f32),
-        ((1, 512), f32),
     ]
     results = tuple(
         jax.ShapeDtypeStruct(shape, f32)
@@ -676,11 +747,13 @@
     )
     made = pl.pallas_call(
         kernel,
-        out_shape=results,
+        out_shape=tuple(
+            pltpu.VMEM(shape, f32) for shape in ((7, 80, 128), (64, 128), (1, 512), (4, 1, 512))
+        ),
         in_specs=[hbm] * 6 + [pl.BlockSpec(memory_space=pltpu.SMEM)],
-        out_specs=(hbm,) * 6,
+        out_specs=(vmem,) * 4,
         scratch_shapes=[pltpu.VMEM(shape, dtype) for shape, dtype in scratch]
-        + [dma((6,)), dma((8,)), dma((8,)), dma((2,)), dma((3,)), dma(()), dma(()), dma((2,)), dma((2,)), dma((6,))],
+        + [dma((6,)), dma((8,)), dma((8,)), dma((2,)), dma((3,)), dma(()), dma(()), dma((2,)), dma((2,))],
         compiler_params=pltpu.CompilerParams(
             collective_id=0, has_side_effects=True, vmem_limit_bytes=56 * 1024 * 1024
         ),
@@ -688,11 +761,10 @@
     return pl.pallas_call(
         handed_on,
         out_shape=results,
-        in_specs=[hbm] * 6,
+        in_specs=[hbm] * 4,
         out_specs=(hbm,) * 6,
         scratch_shapes=[dma((6,))],
-        compiler_params=pltpu.CompilerParams(vmem_limit_bytes=56 * 1024 * 1024),
-    )(*made)
+    )(*(pltpu.with_memory_space_constraint(x, pltpu.VMEM) for x in made))
 
 
 def solution(mesh):

time: 55.2 us -> 42.5 us (0.77)
  Pallas kernels: 54.4 us -> 41.7 us
    pallas_call x2, Pallas kernels: 54.4 us -> 41.7 us  [the longest x1 41 us: local(): pl.pallas_call(kernel, out_shape=tuple((pltpu.VMEM(shape, f32) for shape...]
where the time goes in v3:
time: 42.5 us; the launch traced here: 42.3 us
  Pallas kernels  41.7 us (98%)
  between operations  0.64 us (2%)
    pallas_call x1, Pallas kernels, local(): pl.pallas_call(kernel, out_shape=tuple((pltpu.VMEM(shape, f32) for shape...  41 us

profile of v3, /device:TPU:1, one launch (start us, length us, event | category | flops | bytes accessed | tf_op | source)
XLA Modules:
  0.0 42.3 jit_solution(18125226448251608636)
XLA Ops:
  0.6 41.0 %shard_map.118 = (f32[7,80,128]{2,1,0:T(8,128)S(1)}, f32[64,128]{1,0:T(8,128)S(1)}, f32[1,512]{1,0:T(1,128)S(1)}, f32[4,1,512]{2,1,0:T(1,128)S(1)}) custom-call(f32[64,128]{1,0:T(8,128)} %depth.1, f32[2,64,128]{2,1,0:T(8,128)} %disch.1, f32[4,64,128]{2,1,0:T(8,128)} %sed.1, f32[1,512]{1,0:T(1,128)} %bed.1, s32[64,128]{1,0:T(8,128)} %cmap.1, s32[64,128]{1,0:T(8,128)} %wetm.1, ...), custom_call_target="tpu_custom_call" | custom-call | tf_op jit(solution)/shard_map/pallas_call | solution.py:748
  41.6 0.7 %shard_map.119 = (f32[64,128]{1,0:T(8,128)}, f32[2,64,128]{2,1,0:T(8,128)}, f32[4,64,128]{2,1,0:T(8,128)}, f32[64,128]{1,0:T(8,128)}, f32[1,512]{1,0:T(1,128)}, /*index=5*/f32[4,1,512]{2,1,0:T(1,128)}) custom-call(f32[7,80,128]{2,1,0:T(8,128)S(1)} %get-tuple-element.10.fields, f32[64,128]{1,0:T(8,128)S(1)} %get-tuple-element.11.fine, ...), custom_call_target="tpu_custom_call" | custom-call | tf_op jit(solution)/shard_map/pallas_call | solution.py:761

commit v4 on v3

--- a/solution.py
+++ b/solution.py
@@ -45,9 +45,9 @@
 
 
 def kernel(
-    depth, disch, sed, bed, cmap, wetm, par,
+    depth, disch, sed, bed, cmap, wetm, factors,
     o_fields, o_fine, o_bed, o_dep,
-    nat, raw, bedv, pk, rx, strips, band, band2, cn, nbed, sidx, sshift,
+    params, nat, raw, bedv, pk, rx, strips, band, band2, cn, nbed, sidx, sshift,
     ibuf, rbuf, kbuf, one, two, wet, gx, gy, ox, oy, wd, coef,
     exch, nmain, nside, sel, mhi, mlo, tot, nsum, nrx, rs, wnew,
     in_sem, nb_send, nb_recv, st_send, st_recv, ph_send, ph_recv, ns_send, ns_recv,
@@ -85,6 +85,7 @@
         pltpu.make_async_copy(bed, bedv, in_sem.at[3]),
         pltpu.make_async_copy(cmap, raw.at[0], in_sem.at[4]),
         pltpu.make_async_copy(wetm, raw.at[1], in_sem.at[5]),
+        pltpu.make_async_copy(factors, params, in_sem.at[6]),
     ]
     for copy in loads:
         copy.start()
@@ -141,14 +142,14 @@
             jnp.where(to_lane - from_col == d + 5, 1.0, 0.0).astype(jnp.bfloat16)
         )
 
-    for k in range(FRACTIONS):
-        erode = 0.002 * jnp.full((8, 128), par[2, k], f32)
-        coef[0, k] = 0.05 * jnp.full((8, 128), par[0, k], f32)
-        coef[1, k] = erode / (0.05 * jnp.full((8, 128), par[1, k], f32))
-        coef[2, k] = erode
-
     for copy in loads:
         copy.wait()
+    for k in range(FRACTIONS):
+        erode = 0.002 * jnp.full((8, 128), params[2, k], f32)
+        coef[0, k] = 0.05 * jnp.full((8, 128), params[0, k], f32)
+        coef[1, k] = erode / (0.05 * jnp.full((8, 128), params[1, k], f32))
+        coef[2, k] = erode
+
     nat[8, 8:72, :] = raw[0].astype(f32)
     nat[7, 8:72, :] = raw[1].astype(f32)
 
@@ -302,7 +303,16 @@
             oy[first + n] = 0.05 * planes[n] * turned[n]
             wd[first + n] = 0.2 * planes[n]
 
-    def chunk(src, dst, base, with_bed, start=False):
+    def exchanged(k, mass, s2, settle, w):
+        erosion = jnp.maximum(s2 * coef[1, k] - coef[2, k], 0.0)
+        return coef[0, k] * mass * settle - erosion * w
+
+    def speeds(h, x, y):
+        inv = inverse(jnp.maximum(h, 1.25))
+        u, v = x * inv, y * inv
+        return inv, u, v, u * u + v * v + 1e-6
+
+    def chunk(src, dst, base, with_bed, start=False, count=True):
         kept, diffs = {}, {}
 
         def q_at(q, s):
@@ -323,14 +333,14 @@
             ahead[p] = [
                 tuple(roll(q_at(q, p), step, 1) for step in (1, -1, -2)) for q in range(7)
             ]
-            if not start:
+            if count and not start:
                 ahead[p, "sum"] = [exch[k, base + p] for k in range(FRACTIONS)]
 
         def finish(p, new, turned, changes):
             for q in range(7):
                 dst[q, base + p] = new[q] + turned[q]
-            for k in range(FRACTIONS):
-                exch[k, base + p] = changes[k]
+            for k, value in enumerate(changes):
+                exch[k, base + p] = value
 
         for s in range(-2, 2):
             for q in range(7):
@@ -378,9 +388,7 @@
                 turned.append(roll(flux, 1, 1))
                 new.append(q_at(q, p) - ((fluxes[q, s] - fluxes[q, p]) + flux))
             h = q_at(0, p)
-            inv = inverse(jnp.maximum(h, 1.25))
-            u, v = q_at(1, p) * inv, q_at(2, p) * inv
-            s2 = u * u + v * v + 1e-6
+            inv, u, v, s2 = speeds(h, q_at(1, p), q_at(2, p))
             w = wd[base + p]
             drag = (0.02 * w) * root(s2)
             new[1] = new[1] - drag * u
@@ -391,10 +399,10 @@
             settle = inv * w
             changes = []
             for k in range(FRACTIONS):
-                erosion = jnp.maximum(s2 * coef[1, k] - coef[2, k], 0.0)
-                change = coef[0, k] * q_at(3 + k, p) * settle - erosion * w
+                change = exchanged(k, q_at(3 + k, p), s2, settle, w)
                 new[3 + k] = new[3 + k] - change
-                changes.append(change if start else ahead[p, "sum"][k] + change)
+                if count:
+                    changes.append(change if start else ahead[p, "sum"][k] + change)
             if pending is not None:
                 finish(*pending)
             pending = (p, new, turned, changes)
@@ -438,8 +446,8 @@
     lax.fori_loop(0, 2, early, 0)
 
     await_neighbours((0, 1, 4, 5, 6, 7))
-    slots = [9, *range(1, 9), 12]
-    side_values = [jnp.where(first_eight, rx[0, slot], rx[1, slot]) for slot in slots]
+    groups = [9, *range(1, 9), 12]
+    side_values = [jnp.where(first_eight, rx[0, n], rx[1, n]) for n in groups]
     map_side = jnp.where(first_eight, rx[0, 0], rx[1, 0])
     map_top = jnp.where(first_eight, rx[0, 10], rx[1, 10])
     map_low = jnp.where(first_eight, rx[0, 11], rx[1, 11])
@@ -471,15 +479,6 @@
     def _():
         pltpu.make_async_copy(strips.at[pl.ds(0, 3)], band.at[pl.ds(0, 3)], st_recv.at[2]).wait()
 
-    band_rows = [band[e] for e in range(22)]
-    for e in range(22):
-        band2[e : e + 1, :] = band_rows[e]
-
-    def wide_rows(table, first_row, count):
-        return [
-            jnp.broadcast_to(table[first_row + n : first_row + n + 1, :], (8, 128)) for n in range(count)
-        ]
-
     def looked_up(rows, places):
         found = []
         for g, (index, shift) in enumerate(places):
@@ -498,7 +497,7 @@
             for got, (_, shift) in zip(found, places)
         ]
 
-    rows = wide_rows(band2, 0, 22)
+    rows = [jnp.broadcast_to(band[e], (8, 128)) for e in range(22)]
     groups = [slice(8 * g, 8 * g + 8) for g in range(10)]
     found = looked_up(rows, [(ibuf[r, :], rbuf[r, :]) for r in groups])
     for r, value in zip(groups, found):
@@ -528,23 +527,34 @@
     ghosts(two, False, (1, 2))
     ghosts(two, True, (1, 2))
 
-    for substep in range(1, SUBSTEPS):
-        src, dst = (two, one) if substep % 2 else (one, two)
-
-        def each(c, carry, src=src, dst=dst):
-            chunk(src, dst, MAIN + 5 * c + 4 * (c // 2), True)
+    def step(src, dst, count):
+        def each(c, carry):
+            chunk(src, dst, MAIN + 5 * c + 4 * (c // 2), True, False, count)
             return carry
 
         lax.fori_loop(0, 3, each, 0)
-        if substep < SUBSTEPS - 1:
-            ghosts(dst, False)
-            ghosts(dst, True)
+
+    states = (one, two)
+    for substep in range(1, SUBSTEPS - 1):
+        src, dst = states[substep % 2], states[1 - substep % 2]
+        step(src, dst, True)
+        ghosts(dst, False)
+        ghosts(dst, True)
+    before_last, after_last = states[(SUBSTEPS - 1) % 2], states[SUBSTEPS % 2]
+
+    slots = [*range(MAIN, MAIN + 10), *range(SIDE, SIDE + 5)]
+    totals = {}
+    for slot in slots:
+        h, x, y, *masses = [before_last[q, slot] for q in range(7)]
+        inv, _, _, s2 = speeds(h, x, y)
+        w = wd[slot]
+        for k in range(FRACTIONS):
+            totals[k, slot] = exch[k, slot] + exchanged(k, masses[k], s2, inv * w, w)
 
     edge = jnp.logical_or(lane < 8, lane >= 120)
 
     def natural(planes, n):
-        mains = [planes[MAIN + t] for t in range(10)]
-        sides = [planes[SIDE + t] for t in range(5)]
+        mains, sides = planes[:10], planes[10:]
         turned = [tuple(roll(v, step, 1) for step in (-8, 72, -72, 8)) for v in sides]
         for t, value in enumerate(mains):
             nmain[n, pl.ds(t, 8, stride=10), :] = value
@@ -553,7 +563,7 @@
             nside[n, pl.ds(40 + t, 8, stride=5), :] = jnp.where(low_lanes, c, d)
 
     for k in range(FRACTIONS):
-        natural(exch.at[k], k)
+        natural([totals[k, slot] for slot in slots], k)
     wide_edge = jnp.concatenate([edge, edge], axis=0)
 
     keys = [kbuf[pl.ds(8 + p, 16, stride=4), :] for p in range(4)]
@@ -607,8 +617,9 @@
     lax.fori_loop(0, COLS, send_sums, 0)
     rs[C] = tot[C]
 
+    step(before_last, after_last, False)
     for q in range(7):
-        natural(one.at[q], 4 + q)
+        natural([after_last[q, s] for s in slots], 4 + q)
     for q in range(7):
         for g in range(1, 9):
             rows = slice(8 * g, 8 * g + 8)
@@ -634,9 +645,12 @@
     def _():
         pltpu.make_async_copy(nsum, nrx.at[1], ns_recv.at[1]).wait()
 
-    wnew[1:17, :] = band2[3:19, :] + (nsum[...] + roll(nrx[0], 32, 1) + roll(nrx[1], -32, 1))
+    for e in range(16):
+        band2[e : e + 1, :] = band[3 + e]
+    wnew[1:17, :] = band2[...] + (nsum[...] + roll(nrx[0], 32, 1) + roll(nrx[1], -32, 1))
+    wide = [jnp.broadcast_to(wnew[n : n + 1, :], (8, 128)) for n in range(18)]
     inner = [slice(8 + 8 * g, 16 + 8 * g) for g in range(8)]
-    found = looked_up(wide_rows(wnew, 0, 18), [(ibuf[r, :], rbuf[r, :]) for r in inner])
+    found = looked_up(wide, [(ibuf[r, :], rbuf[r, :]) for r in inner])
     for g, value in enumerate(found):
         o_fine[8 * g : 8 * g + 8, :] = value
 
@@ -712,7 +726,7 @@
         ((2, 13, 8, 128), f32),
         ((16, 1, 128), f32),
         ((22, 1, 128), f32),
-        ((24, 128), f32),
+        ((16, 128), f32),
         ((80, 128), f32),
         ((2, 80, 128), f32),
         ((80, 128), i32),
@@ -750,10 +764,11 @@
         out_shape=tuple(
             pltpu.VMEM(shape, f32) for shape in ((7, 80, 128), (64, 128), (1, 512), (4, 1, 512))
         ),
-        in_specs=[hbm] * 6 + [pl.BlockSpec(memory_space=pltpu.SMEM)],
+        in_specs=[hbm] * 7,
         out_specs=(vmem,) * 4,
-        scratch_shapes=[pltpu.VMEM(shape, dtype) for shape, dtype in scratch]
-        + [dma((6,)), dma((8,)), dma((8,)), dma((2,)), dma((3,)), dma(()), dma(()), dma((2,)), dma((2,))],
+        scratch_shapes=[pltpu.SMEM((3, FRACTIONS), f32)]
+        + [pltpu.VMEM(shape, dtype) for shape, dtype in scratch]
+        + [dma((7,)), dma((8,)), dma((8,)), dma((2,)), dma((3,)), dma(()), dma(()), dma((2,)), dma((2,))],
         compiler_params=pltpu.CompilerParams(
             collective_id=0, has_side_effects=True, vmem_limit_bytes=56 * 1024 * 1024
         ),

time: 42.5 us -> 40.8 us (0.960)
  Pallas kernels: 41.7 us -> 40 us
    pallas_call x1, Pallas kernels: 41 us -> 39.3 us  [local(): pl.pallas_call(kernel, out_shape=tuple((pltpu.VMEM(shape, f32) for shape...]
where the time goes in v4:
time: 40.8 us; the launch traced here: 40.7 us
  Pallas kernels  40 us (98%)
  between operations  0.64 us (2%)
    pallas_call x1, Pallas kernels, local(): pl.pallas_call(kernel, out_shape=tuple((pltpu.VMEM(shape, f32) for shape...  39.3 us

profile of v4, /device:TPU:1, one launch (start us, length us, event | category | flops | bytes accessed | tf_op | source)
XLA Modules:
  0.0 40.7 jit_solution(611270979537739307)
XLA Ops:
  0.6 39.3 %shard_map.118 = (f32[7,80,128]{2,1,0:T(8,128)S(1)}, f32[64,128]{1,0:T(8,128)S(1)}, f32[1,512]{1,0:T(1,128)S(1)}, f32[4,1,512]{2,1,0:T(1,128)S(1)}) custom-call(f32[64,128]{1,0:T(8,128)} %depth.1, f32[2,64,128]{2,1,0:T(8,128)} %disch.1, f32[4,64,128]{2,1,0:T(8,128)} %sed.1, f32[1,512]{1,0:T(1,128)} %bed.1, s32[64,128]{1,0:T(8,128)} %cmap.1, s32[64,128]{1,0:T(8,128)} %wetm.1, ...), custom_call_target="tpu_custom_call" | custom-call | tf_op jit(solution)/shard_map/pallas_call | solution.py:762
  39.9 0.7 %shard_map.119 = (f32[64,128]{1,0:T(8,128)}, f32[2,64,128]{2,1,0:T(8,128)}, f32[4,64,128]{2,1,0:T(8,128)}, f32[64,128]{1,0:T(8,128)}, f32[1,512]{1,0:T(1,128)}, /*index=5*/f32[4,1,512]{2,1,0:T(1,128)}) custom-call(f32[7,80,128]{2,1,0:T(8,128)S(1)} %get-tuple-element.10.fields, f32[64,128]{1,0:T(8,128)S(1)} %get-tuple-element.11.fine, ...), custom_call_target="tpu_custom_call" | custom-call | tf_op jit(solution)/shard_map/pallas_call | solution.py:776

commit v5 on v4

--- a/solution.py
+++ b/solution.py
@@ -57,25 +57,39 @@
     other_half = jnp.where(C < 8, 8, 0)
     barrier = pltpu.get_barrier_semaphore()
 
-    def greet(n, carry):
-        c = (n + other_half) & 15
-        near = jnp.abs(c - C) <= 1
-
-        @pl.when(c != C)
-        def _():
-            pl.semaphore_signal(barrier, inc=1, device_id=(R, c), device_id_type=MESH)
-
-        @pl.when(jnp.logical_and(R > 0, jnp.logical_or(near, c >= COLS - 3)))
-        def _():
-            pl.semaphore_signal(barrier, inc=1, device_id=(R - 1, c), device_id_type=MESH)
-
-        @pl.when(jnp.logical_and(R < ROWS - 1, jnp.logical_or(near, c <= 2)))
-        def _():
-            pl.semaphore_signal(barrier, inc=1, device_id=(R + 1, c), device_id_type=MESH)
-
-        return carry
-
-    lax.fori_loop(0, COLS, greet, 0)
+    others = [other_half + (((C & 7) + k) & 7) for k in (4, 5, 3, 6, 2, 7, 1, 0)]
+    mates = [8 - other_half + (((C & 7) + k) & 7) for k in range(1, 8)]
+    up, down = R > 0, R < ROWS - 1
+    left, right = C > 0, C < COLS - 1
+    both = jnp.logical_and
+
+    def greet(row, c):
+        pl.semaphore_signal(barrier, inc=1, device_id=(row, c), device_id_type=MESH)
+
+    for c in others:
+        greet(R, c)
+
+    @pl.when(down)
+    def _():
+        for c in range(3):
+            greet(R + 1, c)
+
+    @pl.when(up)
+    def _():
+        for c in range(COLS - 3, COLS):
+            greet(R - 1, c)
+
+    for c in mates:
+        greet(R, c)
+    for step in (-1, 0, 1):
+
+        @pl.when(both(down, both(C + step > 2, C + step < COLS)))
+        def _(step=step):
+            greet(R + 1, C + step)
+
+        @pl.when(both(up, both(C + step >= 0, C + step < COLS - 3)))
+        def _(step=step):
+            greet(R - 1, C + step)
 
     mid = pl.ds(8, 64)
     loads = [
@@ -179,9 +193,6 @@
     pk[0] = map_pack
     pk[9] = map_pack
 
-    up, down = R > 0, R < ROWS - 1
-    left, right = C > 0, C < COLS - 1
-    both = jnp.logical_and
     above = jnp.where(C <= 2, COLS, jnp.where(C == COLS - 1, 2, 3))
     below = jnp.where(C >= COLS - 3, COLS, jnp.where(C == 0, 2, 3))
     expected = COLS - 1 + jnp.where(up, above, 0) + jnp.where(down, below, 0)
@@ -220,27 +231,34 @@
             def _(n=n, src=src, dst=dst):
                 pltpu.make_async_copy(src, dst, nb_recv.at[n]).wait()
 
-    def send_strips(n, carry):
-        t = (n + other_half) & 15
-
-        @pl.when(t != C)
-        def _():
-            remote(strips.at[t], band.at[3 + C], st_send.at[0], st_recv.at[0], (R, t)).start()
-
-        @pl.when(both(C <= 2, up))
-        def _():
+    def send_strip(t):
+        remote(strips.at[t], band.at[3 + C], st_send.at[0], st_recv.at[0], (R, t)).start()
+
+    send_to_neighbours((0, 1))
+    for t in others:
+        send_strip(t)
+
+    @pl.when(both(C <= 2, up))
+    def _():
+        def send_up(n, carry):
+            t = (n + other_half) & 15
             remote(strips.at[t], band.at[19 + C], st_send.at[1], st_recv.at[1], (R - 1, t)).start()
-
-        @pl.when(both(C >= COLS - 3, down))
-        def _():
+            return carry
+
+        lax.fori_loop(0, COLS, send_up, 0)
+
+    @pl.when(both(C >= COLS - 3, down))
+    def _():
+        def send_down(n, carry):
+            t = (n + other_half) & 15
             remote(strips.at[t], band.at[C - 13], st_send.at[1], st_recv.at[2], (R + 1, t)).start()
-
-        return carry
-
-    send_to_neighbours((0, 1))
-    lax.fori_loop(0, COLS // 2, send_strips, 0)
+            return carry
+
+        lax.fori_loop(0, COLS, send_down, 0)
+
     send_to_neighbours(range(2, 8))
-    lax.fori_loop(COLS // 2, COLS, send_strips, 0)
+    for t in mates:
+        send_strip(t)
     band[3 + C] = strips[C]
 
     def main_plane(ref, t):
@@ -471,17 +489,9 @@
 
     pltpu.make_async_copy(strips.at[pl.ds(0, 15)], band.at[pl.ds(3, 15)], st_recv.at[0]).wait()
 
-    @pl.when(down)
-    def _():
-        pltpu.make_async_copy(strips.at[pl.ds(0, 3)], band.at[pl.ds(19, 3)], st_recv.at[1]).wait()
-
-    @pl.when(up)
-    def _():
-        pltpu.make_async_copy(strips.at[pl.ds(0, 3)], band.at[pl.ds(0, 3)], st_recv.at[2]).wait()
-
     def looked_up(rows, places):
         found = []
-        for g, (index, shift) in enumerate(places):
+        for g, index, shift in places:
             found.append([
                 jnp.take_along_axis(
                     jnp.where(top_half, rows[2 * g + n], rows[2 * g + n + 1]),
@@ -494,17 +504,31 @@
                 shift == -1, got[0],
                 jnp.where(shift == 0, got[1], jnp.where(shift == 1, got[2], 0.0)),
             )
-            for got, (_, shift) in zip(found, places)
+            for got, (_, _, shift) in zip(found, places)
         ]
 
-    rows = [jnp.broadcast_to(band[e], (8, 128)) for e in range(22)]
-    groups = [slice(8 * g, 8 * g + 8) for g in range(10)]
-    found = looked_up(rows, [(ibuf[r, :], rbuf[r, :]) for r in groups])
-    for r, value in zip(groups, found):
-        nbed[0, r, :] = value
-    found = looked_up(rows, [(sidx[r, :], sshift[r, :]) for r in groups])
-    for r, value in zip(groups, found):
-        nbed[1, r, :] = value
+    def bed_of(groups, rows):
+        span = [slice(8 * g, 8 * g + 8) for g in groups]
+        mains = looked_up(rows, [(g, ibuf[r, :], rbuf[r, :]) for g, r in zip(groups, span)])
+        sides = looked_up(rows, [(g, sidx[r, :], sshift[r, :]) for g, r in zip(groups, span)])
+        for r, a, b in zip(span, mains, sides):
+            nbed[0, r, :] = a
+            nbed[1, r, :] = b
+
+    rows = {e: jnp.broadcast_to(band[e], (8, 128)) for e in range(3, 19)}
+    rows[2], rows[19] = rows[3], rows[18]
+    bed_of(range(1, 9), rows)
+
+    @pl.when(down)
+    def _():
+        pltpu.make_async_copy(strips.at[pl.ds(0, 3)], band.at[pl.ds(19, 3)], st_recv.at[1]).wait()
+
+    @pl.when(up)
+    def _():
+        pltpu.make_async_copy(strips.at[pl.ds(0, 3)], band.at[pl.ds(0, 3)], st_recv.at[2]).wait()
+
+    rows = {e: jnp.broadcast_to(band[e], (8, 128)) for e in (0, 1, 2, 3, 18, 19, 20, 21)}
+    bed_of((0, 9), rows)
 
     bed_main = [main_plane(nbed.at[0], t) for t in range(10)]
     bed_side = side_halo(mixed_rows(nbed.at[1]), 0, side_inner(nbed.at[0]))
@@ -572,39 +596,34 @@
         [jnp.where(wide_edge, nside[k, rows, :], nmain[k, rows, :]) for rows in fourth]
         for k in range(FRACTIONS)
     ]
-    for r in range(3):
-        for d in range(7):
+    for d in range(7):
+        kept = [0.0] * FRACTIONS
+        for r in range(3):
             hits = [keys[p] == r * 7 + d for p in range(4)]
             for k in range(FRACTIONS):
                 acc = jnp.where(hits[0], planes[k][0], 0.0)
                 for p in range(1, 4):
                     acc = acc + jnp.where(hits[p], planes[k][p], 0.0)
-                high = acc.astype(jnp.bfloat16)
-                rows = slice(64 * r + 16 * k, 64 * r + 16 * k + 16)
-                mhi[rows, 128 * d : 128 * d + 128] = high
-                mlo[rows, 128 * d : 128 * d + 128] = (acc - high.astype(f32)).astype(jnp.bfloat16)
+                kept[k] = kept[k] + (acc if r == 1 else roll(acc, r - 1, 0))
+        for k in range(FRACTIONS):
+            high = kept[k].astype(jnp.bfloat16)
+            rows = slice(16 * k, 16 * k + 16)
+            mhi[rows, 128 * d : 128 * d + 128] = high
+            mlo[rows, 128 * d : 128 * d + 128] = (kept[k] - high.astype(f32)).astype(jnp.bfloat16)
     res = jnp.dot(mhi[...], sel[...], preferred_element_type=f32)
-    res = res + jnp.dot(mlo[...], sel[...], preferred_element_type=f32)
-    parts = []
-    for k in range(FRACTIONS):
-        part = res[64 + 16 * k : 80 + 16 * k]
-        part = part + roll(res[16 * k : 16 * k + 16], -1, 0)
-        part = part + roll(res[128 + 16 * k : 144 + 16 * k], 1, 0)
-        parts.append(25.0 * part)
+    res = 25.0 * (res + jnp.dot(mlo[...], sel[...], preferred_element_type=f32))
+    parts = [res[16 * k : 16 * k + 16] for k in range(FRACTIONS)]
     nsum[...] = (parts[0] + parts[1]) + (parts[2] + parts[3])
     for n in range(2):
         pair = parts[2 * n] + roll(parts[2 * n + 1], 64, 1)
         for r in range(COLS):
             tot[r, :, 128 * n : 128 * n + 128] = pair[r : r + 1, :]
 
-    def send_sums(n, carry):
-        r = (n + other_half) & 15
-
-        @pl.when(r != C)
-        def _():
-            remote(tot.at[r], rs.at[C], ph_send, ph_recv, (R, r)).start()
-
-        return carry
+    def send_sum(r):
+        remote(tot.at[r], rs.at[C], ph_send, ph_recv, (R, r)).start()
+
+    for r in others:
+        send_sum(r)
 
     @pl.when(left)
     def _():
@@ -614,7 +633,8 @@
     def _():
         remote(nsum, nrx.at[1], ns_send.at[1], ns_recv.at[1], (R, C + 1)).start()
 
-    lax.fori_loop(0, COLS, send_sums, 0)
+    for r in mates:
+        send_sum(r)
     rs[C] = tot[C]
 
     step(before_last, after_last, False)
@@ -650,7 +670,7 @@
     wnew[1:17, :] = band2[...] + (nsum[...] + roll(nrx[0], 32, 1) + roll(nrx[1], -32, 1))
     wide = [jnp.broadcast_to(wnew[n : n + 1, :], (8, 128)) for n in range(18)]
     inner = [slice(8 + 8 * g, 16 + 8 * g) for g in range(8)]
-    found = looked_up(wide, [(ibuf[r, :], rbuf[r, :]) for r in inner])
+    found = looked_up(wide, [(g, ibuf[r, :], rbuf[r, :]) for g, r in enumerate(inner)])
     for g, value in enumerate(found):
         o_fine[8 * g : 8 * g + 8, :] = value
 
@@ -747,8 +767,8 @@
         ((11, 80, 128), f32),
         ((11, 80, 128), f32),
         ((896, 128), bf16),
-        ((192, 896), bf16),
-        ((192, 896), bf16),
+        ((64, 896), bf16),
+        ((64, 896), bf16),
         ((16, 1, 256), f32),
         ((16, 128), f32),
         ((2, 16, 128), f32),

time: 40.8 us -> 40.6 us (level)
  no operation moved by 1% of the time
where the time goes in v5:
time: 40.6 us; the launch traced here: 40.4 us
  Pallas kernels  39.8 us (98%)
  between operations  0.64 us (2%)
    pallas_call x1, Pallas kernels, local(): pl.pallas_call(kernel, out_shape=tuple((pltpu.VMEM(shape, f32) for shape...  39 us

profile of v5, /device:TPU:1, one launch (start us, length us, event | category | flops | bytes accessed | tf_op | source)
XLA Modules:
  0.0 40.4 jit_solution(11683653719076529325)
XLA Ops:
  0.6 39.0 %shard_map.118 = (f32[7,80,128]{2,1,0:T(8,128)S(1)}, f32[64,128]{1,0:T(8,128)S(1)}, f32[1,512]{1,0:T(1,128)S(1)}, f32[4,1,512]{2,1,0:T(1,128)S(1)}) custom-call(f32[64,128]{1,0:T(8,128)} %depth.1, f32[2,64,128]{2,1,0:T(8,128)} %disch.1, f32[4,64,128]{2,1,0:T(8,128)} %sed.1, f32[1,512]{1,0:T(1,128)} %bed.1, s32[64,128]{1,0:T(8,128)} %cmap.1, s32[64,128]{1,0:T(8,128)} %wetm.1, ...), custom_call_target="tpu_custom_call" | custom-call | tf_op jit(solution)/shard_map/pallas_call | solution.py:782
  39.7 0.7 %shard_map.119 = (f32[64,128]{1,0:T(8,128)}, f32[2,64,128]{2,1,0:T(8,128)}, f32[4,64,128]{2,1,0:T(8,128)}, f32[64,128]{1,0:T(8,128)}, f32[1,512]{1,0:T(1,128)}, /*index=5*/f32[4,1,512]{2,1,0:T(1,128)}) custom-call(f32[7,80,128]{2,1,0:T(8,128)S(1)} %get-tuple-element.10.fields, f32[64,128]{1,0:T(8,128)S(1)} %get-tuple-element.11.fine, ...), custom_call_target="tpu_custom_call" | custom-call | tf_op jit(solution)/shard_map/pallas_call | solution.py:796

commit v6 on v5

--- a/solution.py
+++ b/solution.py
@@ -238,27 +238,26 @@
     for t in others:
         send_strip(t)
 
-    @pl.when(both(C <= 2, up))
-    def _():
-        def send_up(n, carry):
-            t = (n + other_half) & 15
-            remote(strips.at[t], band.at[19 + C], st_send.at[1], st_recv.at[1], (R - 1, t)).start()
-            return carry
-
-        lax.fori_loop(0, COLS, send_up, 0)
-
-    @pl.when(both(C >= COLS - 3, down))
-    def _():
-        def send_down(n, carry):
-            t = (n + other_half) & 15
-            remote(strips.at[t], band.at[C - 13], st_send.at[1], st_recv.at[2], (R + 1, t)).start()
-            return carry
-
-        lax.fori_loop(0, COLS, send_down, 0)
-
+    def send_beyond(targets):
+        @pl.when(both(C <= 2, up))
+        def _():
+            for t in targets:
+                remote(
+                    strips.at[t], band.at[19 + C], st_send.at[1], st_recv.at[1], (R - 1, t)
+                ).start()
+
+        @pl.when(both(C >= COLS - 3, down))
+        def _():
+            for t in targets:
+                remote(
+                    strips.at[t], band.at[C - 13], st_send.at[1], st_recv.at[2], (R + 1, t)
+                ).start()
+
+    send_beyond(others)
     send_to_neighbours(range(2, 8))
     for t in mates:
         send_strip(t)
+    send_beyond([*mates, C])
     band[3 + C] = strips[C]
 
     def main_plane(ref, t):

time: 40.6 us -> 40.5 us (level)
  no operation moved by 1% of the time
where the time goes in v6:
time: 40.5 us; the launch traced here: 40.4 us
  Pallas kernels  39.8 us (98%)
  between operations  0.64 us (2%)
    pallas_call x1, Pallas kernels, local(): pl.pallas_call(kernel, out_shape=tuple((pltpu.VMEM(shape, f32) for shape...  39 us

profile of v6, /device:TPU:1, one launch (start us, length us, event | category | flops | bytes accessed | tf_op | source)
XLA Modules:
  0.0 40.4 jit_solution(17943624966775160711)
XLA Ops:
  0.6 39.0 %shard_map.118 = (f32[7,80,128]{2,1,0:T(8,128)S(1)}, f32[64,128]{1,0:T(8,128)S(1)}, f32[1,512]{1,0:T(1,128)S(1)}, f32[4,1,512]{2,1,0:T(1,128)S(1)}) custom-call(f32[64,128]{1,0:T(8,128)} %depth.1, f32[2,64,128]{2,1,0:T(8,128)} %disch.1, f32[4,64,128]{2,1,0:T(8,128)} %sed.1, f32[1,512]{1,0:T(1,128)} %bed.1, s32[64,128]{1,0:T(8,128)} %cmap.1, s32[64,128]{1,0:T(8,128)} %wetm.1, ...), custom_call_target="tpu_custom_call" | custom-call | tf_op jit(solution)/shard_map/pallas_call | solution.py:781
  39.7 0.7 %shard_map.119 = (f32[64,128]{1,0:T(8,128)}, f32[2,64,128]{2,1,0:T(8,128)}, f32[4,64,128]{2,1,0:T(8,128)}, f32[64,128]{1,0:T(8,128)}, f32[1,512]{1,0:T(1,128)}, /*index=5*/f32[4,1,512]{2,1,0:T(1,128)}) custom-call(f32[7,80,128]{2,1,0:T(8,128)S(1)} %get-tuple-element.10.fields, f32[64,128]{1,0:T(8,128)S(1)} %get-tuple-element.11.fine, ...), custom_call_target="tpu_custom_call" | custom-call | tf_op jit(solution)/shard_map/pallas_call | solution.py:795
